TPU v7x, 32 devices: a whole 2x2x4 slice. The times are simulated.
32 devices in a mesh: trial: 2 (over y), freq: 4 (over z), acc: 4 (over x, core).
Axes of the slice: x: 2, y: 2, z: 4, core: 2. Of those that a mesh axis runs over, the one named last changes fastest.
Arguments:
- spectrum: bfloat16 [2, 8192], P(None, ('trial', 'freq')), parts along dimension 1, may hold values from -6 to 6
- templates: bfloat16 [2, 200, 384], P(None, 'acc'), may hold values from -0.15625 to 0.15625
- offsets: int32 [200], P('acc'), may hold values from 0 to 127
Outputs:
- harmonic_sum: float32 [200, 8192], P(None, ('trial', 'freq', 'acc')), parts along dimension 1
There are 2 independent parts, one for each index of `trial`. A program takes and returns all parts, laid end to end along the dimension named above; an argument that names none is the same for every part. Nothing has to cross between parts.
All inputs are finite; a program needn't handle non-finite values.
Results may differ from a plain program's by a relative error of at most 0.0033.
Values may be sent and summed in bfloat16 or wider, within the bound.
No kernel may reach another device: no remote copies, remote signals or barrier semaphores. Data moves between devices by JAX's collectives and lax.ppermute only.
A program may use at most 64 MiB of HBM per device.

v0:
```python
import jax
import jax.numpy as jnp
from jax import lax
from jax.sharding import PartitionSpec as P

Z = 200
K = 384
OFF = 128
H = 8


def passed_along(value, axis, by):
    devices = lax.axis_size(axis)
    pairs = [(i, i + by) for i in range(devices) if 0 <= i + by < devices]
    return lax.ppermute(value, axis, pairs)


def for_sending(value):
    return jax.tree.map(lambda a: a.astype(jnp.bfloat16) if a.dtype == jnp.float32 else a, value)


def shifted_templates(templates, offsets, width):

    def place_row(template_row, start_col):
        zero_row = jnp.zeros((2, width), templates.dtype)
        return lax.dynamic_update_slice(zero_row, template_row, (jnp.int32(0), start_col))

    return jax.vmap(place_row, in_axes=(1, 0), out_axes=1)(templates, offsets)


def conv_kernel(shifted):
    real_part = shifted[0]
    imag_part = shifted[1]
    upper = jnp.stack([real_part, -imag_part], axis=1)
    lower = jnp.stack([imag_part, real_part], axis=1)
    return jnp.concatenate([upper, lower], axis=0)


def correlate_power(kernel, line, stride, out_len):
    product = lax.conv_general_dilated(
        line[None],
        kernel,
        (stride,),
        "VALID",
        dimension_numbers=("NCH", "OIH", "NCH"),
        preferred_element_type=jnp.float32,
    )[0]
    product = product[:, :out_len]
    half_rows = kernel.shape[0] // 2
    real_out = product[:half_rows]
    imag_out = product[half_rows:]
    return (real_out * real_out + imag_out * imag_out).astype(jnp.bfloat16)


def harmonic_rows(harmonic):
    centre = Z // 2
    row_low = centre - centre // harmonic
    row_high = centre + (Z - 1 - centre) // harmonic
    return (row_low, row_high - row_low + 1, centre - harmonic * (centre // harmonic))


def place_rows(result, partial_value, row_low, row_count):
    return result + jnp.pad(partial_value, ((row_low, Z - row_low - row_count), (0, 0)))


def decimate(full_plane, harmonic, freq_index, slab_bins, sub_bins):
    row_low, row_count, row_first = harmonic_rows(harmonic)
    row_block = full_plane[row_first : row_first + harmonic * (row_count - 1) + 1 : harmonic]
    length = slab_bins // harmonic + 1
    start_col = (harmonic - freq_index * slab_bins % harmonic) % harmonic
    widened = jnp.pad(row_block, ((0, 0), (0, harmonic * length + harmonic - slab_bins)))
    picked = lax.dynamic_slice_in_dim(widened, start_col, harmonic * length, 1)
    picked = picked.reshape(row_count, length, harmonic)[:, :, 0]
    fund_base = (freq_index * slab_bins + start_col) // harmonic
    return (jnp.pad(picked, ((0, 0), (sub_bins, sub_bins))), fund_base, length)


def take_window(decimated, fund_base, length, target, acc_index, slab_bins, sub_bins):
    offset = jnp.clip(
        target * slab_bins + acc_index * sub_bins - fund_base + sub_bins, 0, length + sub_bins
    )
    return lax.dynamic_slice_in_dim(decimated, offset, sub_bins, 1)


def shards(spectrum, templates, offsets):
    freq_count = lax.axis_size("freq")
    acc_count = lax.axis_size("acc")
    freq_index = lax.axis_index("freq")
    acc_index = lax.axis_index("acc")
    slab_bins = spectrum.shape[1]
    sub_bins = slab_bins // acc_count
    window_width = K + OFF
    result = jnp.zeros((Z, sub_bins), jnp.float32)
    following = passed_along(spectrum[:, : window_width - 1], "freq", -1)
    extended = jnp.concatenate([spectrum, following], axis=1)
    kernel = conv_kernel(shifted_templates(templates, offsets, window_width))
    own_rows = correlate_power(kernel, extended, 1, slab_bins)
    full_plane = lax.all_gather(own_rows, "acc", axis=0, tiled=True)
    local_part = lax.dynamic_slice_in_dim(full_plane, acc_index * sub_bins, sub_bins, 1)
    result = result + local_part.astype(jnp.float32)
    targets = jnp.arange(freq_count, dtype=jnp.int32)
    slot_list = []
    layout = []
    for harmonic in range(2, H + 1):
        decimated, fund_base, length = decimate(
            full_plane, harmonic, freq_index, slab_bins, sub_bins
        )
        row_low, row_count, row_first = harmonic_rows(harmonic)
        layout.append((row_low, row_count))

        def slot_for(target, decimated=decimated, fund_base=fund_base, length=length):
            return take_window(decimated, fund_base, length, target, acc_index, slab_bins, sub_bins)

        slot_list.append(jax.vmap(slot_for)(targets))
    outgoing = jnp.concatenate(slot_list, axis=1)
    incoming = lax.all_to_all(
        for_sending(outgoing), "freq", split_axis=0, concat_axis=0, tiled=True
    ).astype(outgoing.dtype)
    summed = jnp.sum(incoming, axis=0, dtype=jnp.float32)
    row_offset = 0
    for row_low, row_count in layout:
        result = place_rows(result, summed[row_offset : row_offset + row_count], row_low, row_count)
        row_offset = row_offset + row_count
    return result


def solution(mesh):
    return jax.shard_map(
        shards,
        mesh=mesh,
        in_specs=(P(None, ("trial", "freq")), P(None, "acc", None), P("acc")),
        out_specs=P(None, ("trial", "freq", "acc")),
        check_vma=False,
    )
```

profile of v0, /device:TPU:0, one launch (start us, length us, event | category | flops | bytes accessed | tf_op | source)
XLA Modules:
  0.0 531.7 jit_solution(16656636649837620168)
XLA Ops:
  2.9 398.8 %while.15 = (s32[]{:T(128)}, bf16[50,2,512]{2,1,0:T(2,128)(2,1)S(1)}, s32[50,3]{0,1:T(4,128)S(1)}, bf16[50,2,384]{2,1,0:T(2,128)(2,1)}, s32[]{:T(128)}, /*index=5*/s32[3]{0:T(128)}, s32[]{:T(128)}) while((s32[]{:T(128)}, bf16[50,2,512]{2,1,0:T(2,128)(2,1)S(1)}, s32[50,3]{0,1:T(4,128)S(1)}, bf16[50,2,384]{2,1,0:T(2,128)(2,1)}, s32[]{:T(128)}, ...), condition=%wide.while_cond.7, body=%wide.while_body.7.sunk | while | flops 787 | bytes 7851 | solution.py:26
  3.5 3.3 and_reduce_fusion.2
  11.5 3.3 and_reduce_fusion.2
  19.5 3.3 and_reduce_fusion.2
  27.4 3.3 and_reduce_fusion.2
  35.4 3.3 and_reduce_fusion.2
  43.4 3.3 and_reduce_fusion.2
  51.4 3.3 and_reduce_fusion.2
  59.4 3.3 and_reduce_fusion.2
  67.3 3.3 and_reduce_fusion.2
  75.3 3.3 and_reduce_fusion.2
  83.3 3.3 and_reduce_fusion.2
  403.7 36.2 %fusion.10 = f32[1,100,1024]{1,0,2:T(1,128)S(1)} fusion(bf16[1,2,1535]{1,0,2:T(2,128)(2,1)S(1)} %copy.99, bf16[100,2,512]{0,1,2:T(2,128)(2,1)S(1)} %copy.100), kind=kOutput, calls=%fused_computation.57 | convolution fusion | flops 209715200 | bytes 620540 | tf_op jit(solution)/shard_map/conv_general_dilated | solution.py:40
  442.0 10.2 %all-gather = bf16[1,200,1024]{2,0,1:T(2,128)(2,1)S(1)} all-gather(bf16[1,50,1024]{2,0,1:T(2,128)(2,1)S(1)} %add_convert_fusion), channel_id=2, replica_groups=mesh['trial'=2,'freq'=4,'acc'=4] {'acc'}, dimensions={1}, use_global_device_ids=true | all-gather | bytes 512000 | tf_op jit(solution)/shard_map/all_gather | solution.py:98
  455.1 5.8 %while.14 = (s32[]{:T(128)}, bf16[25,641]{1,0:T(8,128)(2,1)S(1)}, s32[4,2]{0,1:T(2,128)S(1)}, bf16[4,25,256]{2,1,0:T(8,128)(2,1)S(1)}, s32[]{:T(128)}) while((s32[]{:T(128)}, bf16[25,641]{1,0:T(8,128)(2,1)S(1)}, s32[4,2]{0,1:T(2,128)S(1)}, bf16[4,25,256]{2,1,0:T(8,128)(2,1)S(1)}, s32[]{:T(128)}) %tuple.130), condition=%wide.while_cond.6, body=%wide.while_body.6.sunk | while | flops 2 | bytes 32865 | solution.py:82
  461.5 4.8 while.13
  467.0 5.3 %while.10 = (s32[]{:T(128)}, bf16[50,769]{1,0:T(8,128)(2,1)S(1)}, s32[4,2]{0,1:T(2,128)S(1)}, bf16[4,50,256]{2,1,0:T(8,128)(2,1)S(1)}, s32[]{:T(128)}) while((s32[]{:T(128)}, bf16[50,769]{1,0:T(8,128)(2,1)S(1)}, s32[4,2]{0,1:T(2,128)S(1)}, bf16[4,50,256]{2,1,0:T(8,128)(2,1)S(1)}, s32[]{:T(128)}) %tuple.118), condition=%wide.while_cond.2, body=%wide.while_body.2.sunk | while | flops 2 | bytes 57441 | solution.py:82
  473.1 5.4 %while.9 = (s32[]{:T(128)}, bf16[67,854]{1,0:T(8,128)(2,1)S(1)}, s32[4,2]{0,1:T(2,128)S(1)}, bf16[4,67,256]{2,1,0:T(8,128)(2,1)S(1)}, s32[]{:T(128)}) while((s32[]{:T(128)}, bf16[67,854]{1,0:T(8,128)(2,1)S(1)}, s32[4,2]{0,1:T(2,128)S(1)}, bf16[4,67,256]{2,1,0:T(8,128)(2,1)S(1)}, s32[]{:T(128)}) %tuple.115), condition=%wide.while_cond.1, body=%wide.while_body.1.sunk | while | flops 2 | bytes 73825 | solution.py:82
  479.2 5.4 %while.11 = (s32[]{:T(128)}, bf16[40,717]{1,0:T(8,128)(2,1)S(1)}, s32[4,2]{0,1:T(2,128)S(1)}, bf16[4,40,256]{2,1,0:T(8,128)(2,1)S(1)}, s32[]{:T(128)}) while((s32[]{:T(128)}, bf16[40,717]{1,0:T(8,128)(2,1)S(1)}, s32[4,2]{0,1:T(2,128)S(1)}, bf16[4,40,256]{2,1,0:T(8,128)(2,1)S(1)}, s32[]{:T(128)}) %tuple.121), condition=%wide.while_cond.3, body=%wide.while_body.3.sunk | while | flops 2 | bytes 41057 | solution.py:82
  485.2 5.0 while.12
  491.1 5.4 %while.8 = (s32[]{:T(128)}, bf16[100,1025]{1,0:T(8,128)(2,1)S(1)}, s32[4,2]{0,1:T(2,128)S(1)}, bf16[4,100,256]{2,1,0:T(8,128)(2,1)S(1)}, s32[]{:T(128)}) while((s32[]{:T(128)}, bf16[100,1025]{1,0:T(8,128)(2,1)S(1)}, s32[4,2]{0,1:T(2,128)S(1)}, bf16[4,100,256]{2,1,0:T(8,128)(2,1)S(1)}, s32[]{:T(128)}) %tuple.112), condition=%wide.while_cond, body=%wide.while_body.sunk | while | flops 2 | bytes 106593 | solution.py:82
  496.5 9.4 %concatenate.43 = bf16[4,344,256]{2,1,0:T(8,128)(2,1)} concatenate(bf16[4,100,256]{2,1,0:T(8,128)(2,1)S(1)} %get-tuple-element.12, bf16[4,67,256]{2,1,0:T(8,128)(2,1)S(1)} %get-tuple-element.20, bf16[4,50,256]{2,1,0:T(8,128)(2,1)S(1)} %get-tuple-element.28, bf16[4,40,256]{2,1,0:T(8,128)(2,1)S(1)} %get-tuple-element.36, bf16[4,33,256]{2,1,0:T(8,128)(2,1)S(1)} %get-tuple-element.44, ...), dimensions={1} | concatenate | bytes 1409024 | tf_op jit(solution)/shard_map/concatenate | solution.py:115
  506.0 5.9 %all-to-all-start = ((bf16[4,344,256]{2,1,0:T(8,128)(2,1)}), bf16[4,344,256]{2,1,0:T(8,128)(2,1)S(1)}, u32[]{:S(2)}, u32[]{:S(2)}) async-start(bf16[4,344,256]{2,1,0:T(8,128)(2,1)} %concatenate.43), calls=%async_computation | async-start | bytes 1409024 | tf_op jit(solution)/shard_map/all_to_all | solution.py:116
  512.1 18.7 %all-to-all-done = bf16[4,344,256]{2,1,0:T(8,128)(2,1)S(1)} async-done(((bf16[4,344,256]{2,1,0:T(8,128)(2,1)}), bf16[4,344,256]{2,1,0:T(8,128)(2,1)S(1)}, u32[]{:S(2)}, u32[]{:S(2)}) %all-to-all-start) | async-done | bytes 704544 | tf_op jit(solution)/shard_map/all_to_all | solution.py:116
  (421 shorter events, 412.9 us)
Async XLA Ops:
  0.7 401.9 %collective-permute-start = (bf16[2,511]{1,0:T(2,128)(2,1)S(1)}, bf16[2,511]{1,0:T(2,128)(2,1)S(1)}, u32[]{:S(2)}, u32[]{:S(2)}) collective-permute-start(bf16[2,511]{1,0:T(2,128)(2,1)S(1)} %slice.80), channel_id=1, source_target_pairs={{4,0},{8,4},{12,8},{5,1},{9,5},{13,9},{6,2},{10,6},{14,10},{7,3},{... | collective-permute-start | bytes 6140 | tf_op jit(solution)/shard_map/ppermute | solution.py:15
  401.7 0.9 copy-start
  506.0 24.8 %all-to-all-start = ((bf16[4,344,256]{2,1,0:T(8,128)(2,1)}), bf16[4,344,256]{2,1,0:T(8,128)(2,1)S(1)}, u32[]{:S(2)}, u32[]{:S(2)}) async-start(bf16[4,344,256]{2,1,0:T(8,128)(2,1)} %concatenate.43), calls=%async_computation | async-start | bytes 1409024 | tf_op jit(solution)/shard_map/all_to_all | solution.py:116
where the time goes:
time: 538 us; the launch traced here: 532 us
  other arithmetic  293 us (54%)
  local copies, waits for them, and re-layouts  164 us (30%)
  matrix products  36.2 us (7%)
  waiting for transfers between devices  18.7 us (3%)
  blocking collectives  10.2 us (2%)
  starting transfers between devices  7.21 us (1%)
    scatter x100, other arithmetic  291 us
    scatter x150, local copies, waits for them, and re-layouts  106 us
    gather x84, local copies, waits for them, and re-layouts  36.9 us
    conv_general_dilated x1, matrix products, correlate_power(): lax.conv_general_dilated(line[None], kernel, (stride,), 'VALID', dimensio...  36.2 us
    all_to_all x1, waiting for transfers between devices, shards(): lax.all_to_all(for_sending(outgoing), 'freq', split_axis=0, concat_axis=0...  18.7 us
  transfers between devices with their start and end apart: 2, of which 1 were waited for; matrix products, arithmetic and copies ran while one was open for 75% of the time, Pallas kernels for 0%

commit v1 on v0

v1 whole, which is shorter than its diff:
```python
import functools

import jax
import jax.numpy as jnp
from jax import lax
from jax.experimental import pallas as pl
from jax.experimental.pallas import tpu as pltpu
from jax.sharding import PartitionSpec as P

K = 384
OFF = 128
H = 8
LANES = 128
WIDTH = K + OFF
NT = (((1,), (1,)), ((), ()))
VMEM = pl.BlockSpec(memory_space=pltpu.VMEM)


def round_up(value, step):
    return (value + step - 1) // step * step


def row_blocks(rows):
    centre = rows // 2
    blocks = []
    for harmonic in range(1, H + 1):
        low = centre - centre // harmonic
        end = centre + (rows - 1 - centre) // harmonic + 1
        start = low // 16 * 16
        blocks.append((start, round_up(end, 16) - start))
    return blocks


def lane_gather(values, index):
    return jnp.take_along_axis(values, index, axis=1, mode="promise_in_bounds")


def shift_kernel(offsets_ref, templates_ref, out_ref):
    rows = templates_ref.shape[1]
    padded = out_ref.shape[1]
    taps = templates_ref.shape[2] // LANES
    spot = lax.broadcasted_iota(jnp.int32, (padded, rows), 0) == lax.broadcasted_iota(jnp.int32, (padded, rows), 1)
    offset = jnp.sum(jnp.where(spot, offsets_ref[...].astype(jnp.float32), 0.0), axis=1, keepdims=True)
    offset = jnp.broadcast_to(offset.astype(jnp.int32), (padded, LANES))
    lane = lax.broadcasted_iota(jnp.int32, (padded, LANES), 1)
    index = (lane - offset) & (LANES - 1)
    stays = lane >= offset
    for part in range(2):
        before = jnp.zeros((padded, LANES), jnp.float32)
        for tile in range(taps + 1):
            if tile < taps:
                values = templates_ref[part, :, tile * LANES : (tile + 1) * LANES].astype(jnp.float32)
                values = jnp.concatenate([values, jnp.zeros((padded - rows, LANES), jnp.float32)], axis=0)
                turned = lane_gather(values, index)
            else:
                turned = jnp.zeros((padded, LANES), jnp.float32)
            placed = jnp.where(stays, turned, before)
            out_ref[part, :, tile * LANES : (tile + 1) * LANES] = placed.astype(jnp.bfloat16)
            before = turned


def shift_templates(offsets, templates):
    parts, rows, _ = templates.shape
    return pl.pallas_call(
        shift_kernel,
        out_shape=jax.ShapeDtypeStruct((parts, round_up(rows, 16), WIDTH), jnp.bfloat16),
        in_specs=[VMEM, VMEM],
        out_specs=VMEM,
        name="shift_templates",
    )(offsets.reshape(1, rows), templates)


def harmonic_kernel(*refs, n_slabs, masks, shard_rows, rows):
    slabs = refs[:n_slabs]
    shards = refs[n_slabs : n_slabs + len(masks)]
    out_ref, line, windows, taps, picked, total = refs[n_slabs + len(masks) :]
    sub_bins = out_ref.shape[1]
    blocks_f = sub_bins // LANES
    window_tiles = WIDTH // LANES
    padded = shards[0].shape[1]
    slab_tiles = slabs[0].shape[1] // LANES
    filled = n_slabs * slab_tiles
    freq_index = lax.axis_index("freq")
    acc_index = lax.axis_index("acc")

    line[:, filled:, :] = jnp.zeros((2, line.shape[1] - filled, LANES), jnp.float32)
    for slot, slab in enumerate(slabs):
        values = slab[...].astype(jnp.float32)
        for tile in range(slab_tiles):
            for part in range(2):
                line[part, pl.ds(slot * slab_tiles + tile, 1), :] = values[part : part + 1, tile * LANES : (tile + 1) * LANES]

    for slot, shard in enumerate(shards):
        for part in range(2):
            taps[slot * padded : (slot + 1) * padded, part * WIDTH : (part + 1) * WIDTH] = shard[part]

    centre = rows // 2
    column = lax.broadcasted_iota(jnp.int32, (1, taps.shape[0]), 1)
    row_at = jnp.full(column.shape, -H * rows, jnp.int32)
    for slot, mask in enumerate(masks):
        inside = (column >= slot * padded) & (column < slot * padded + shard_rows)
        row_at = jnp.where(inside, (acc_index ^ mask) * shard_rows + column - slot * padded, row_at)
    blocks = row_blocks(rows)
    at = 0
    for harmonic in range(1, H + 1):
        start, count = blocks[harmonic - 1]
        row = lax.broadcasted_iota(jnp.int32, (count, taps.shape[0]), 0) + start
        choose = jnp.where(centre + harmonic * (row - centre) == row_at, 1.0, 0.0).astype(jnp.bfloat16)
        chosen = jnp.dot(choose, taps[...], preferred_element_type=jnp.float32).astype(jnp.bfloat16)
        picked[at : at + count, :] = chosen[:, :WIDTH]
        picked[at + count : at + 2 * count, :] = chosen[:, WIDTH:]
        at += 2 * count

    lane = lax.broadcasted_iota(jnp.int32, (16, LANES), 1)
    sublane = lax.broadcasted_iota(jnp.int32, (16, LANES), 0)
    total[...] = jnp.zeros_like(total)
    at = 0
    for harmonic in range(1, H + 1):
        place = lane + harmonic * sublane
        index = place & (LANES - 1)
        stays = place < LANES
        n_tiles = window_tiles + harmonic * blocks_f
        first = ((harmonic - 1) * freq_index * slab_tiles) + harmonic * acc_index * blocks_f
        first = jnp.minimum(first, filled)
        for part in range(2):
            turned = []
            for tile in range(n_tiles + 1):
                values = jnp.broadcast_to(line[part, pl.ds(first + tile, 1), :], (16, LANES))
                turned.append(lane_gather(values, index))
            base = [jnp.where(stays, turned[t], turned[t + 1]).astype(jnp.bfloat16) for t in range(n_tiles)]
            moved = {0: base}
            for group in range(LANES // 16):
                tile_by, lane_by = divmod(16 * harmonic * group, LANES)
                if lane_by not in moved:
                    rolled = [pltpu.roll(values, LANES - lane_by, 1) for values in base]
                    keep = lane < LANES - lane_by
                    moved[lane_by] = [jnp.where(keep, rolled[t], rolled[min(t + 1, n_tiles - 1)]) for t in range(n_tiles)]
                for block in range(blocks_f):
                    for tile in range(window_tiles):
                        row = block * LANES + 16 * group
                        windows[harmonic - 1, part, row : row + 16, tile * LANES : (tile + 1) * LANES] = moved[lane_by][
                            tile_by + harmonic * block + tile
                        ]
        start, count = blocks[harmonic - 1]
        chosen = picked[at : at + 2 * count, :]
        at += 2 * count
        with_real = lax.dot_general(chosen, windows[harmonic - 1, 0], NT, preferred_element_type=jnp.float32)
        with_imag = lax.dot_general(chosen, windows[harmonic - 1, 1], NT, preferred_element_type=jnp.float32)
        real = with_real[:count] - with_imag[count:]
        imag = with_imag[:count] + with_real[count:]
        power = (real * real + imag * imag).astype(jnp.bfloat16)
        total[start : start + count, :] += power.astype(jnp.float32)
    out_ref[...] = total[:rows, :]


def harmonic_sums(slabs, shards, masks, shard_rows, rows, sub_bins):
    padded = shards[0].shape[1]
    filled = len(slabs) * slabs[0].shape[1] // LANES
    beyond = WIDTH // LANES + H * (sub_bins // LANES) + 1
    picked_rows = 2 * sum(count for _, count in row_blocks(rows))
    return pl.pallas_call(
        functools.partial(harmonic_kernel, n_slabs=len(slabs), masks=masks, shard_rows=shard_rows, rows=rows),
        out_shape=jax.ShapeDtypeStruct((rows, sub_bins), jnp.float32),
        in_specs=[VMEM] * (len(slabs) + len(shards)),
        out_specs=VMEM,
        scratch_shapes=[
            pltpu.VMEM((2, filled + beyond, LANES), jnp.float32),
            pltpu.VMEM((H, 2, sub_bins, WIDTH), jnp.bfloat16),
            pltpu.VMEM((len(shards) * padded, 2 * WIDTH), jnp.bfloat16),
            pltpu.VMEM((picked_rows, WIDTH), jnp.bfloat16),
            pltpu.VMEM((round_up(rows, 16), sub_bins), jnp.float32),
        ],
        compiler_params=pltpu.CompilerParams(vmem_limit_bytes=32 << 20),
        name="harmonic_sums",
    )(*slabs, *shards)


def shards(spectrum, templates, offsets):
    freq_count = lax.axis_size("freq")
    acc_count = lax.axis_size("acc")
    shard_rows = templates.shape[1]
    slabs = [spectrum]
    for by in range(1, freq_count):
        slabs.append(lax.ppermute(spectrum, "freq", [(i, i - by) for i in range(by, freq_count)]))
    held = [shift_templates(offsets, templates)]
    masks = [0]
    step = acc_count // 2
    while step >= 1:
        pairs = [(i, i ^ step) for i in range(acc_count)]
        held = held + [lax.ppermute(shard, "acc", pairs) for shard in held]
        masks = masks + [mask ^ step for mask in masks]
        step //= 2
    return harmonic_sums(slabs, held, masks, shard_rows, acc_count * shard_rows, spectrum.shape[1] // acc_count)


def solution(mesh):
    return jax.shard_map(
        shards,
        mesh=mesh,
        in_specs=(P(None, ("trial", "freq")), P(None, "acc", None), P("acc")),
        out_specs=P(None, ("trial", "freq", "acc")),
        check_vma=False,
    )
```

time: 538 us -> 25.5 us (0.05); the launches traced: 532 us -> 25.3 us
  other arithmetic: 293 us -> 0 us
  local copies, waits for them, and re-layouts: 164 us -> 2.44 us
  matrix products: 36.2 us -> 0 us
  blocking collectives: 10.2 us -> 0 us
  waiting for transfers between devices: 18.7 us -> 10.9 us
    scatter x101 -> x0, other arithmetic: 291 us -> none
    scatter x151 -> x0, local copies, waits for them, and re-layouts: 106 us -> none
    gather x84 -> x0, local copies, waits for them, and re-layouts: 36.9 us -> none
    conv_general_dilated x1 -> x0, matrix products: 36.2 us -> none  [correlate_power(): lax.conv_general_dilated(line[None], kernel, (stride,), 'VALID', dimensio...]
    all_to_all x1 -> x0, waiting for transfers between devices: 18.7 us -> none  [shards(): lax.all_to_all(for_sending(outgoing), 'freq', split_axis=0, concat_axis=0...]
    ppermute x1 -> x6, waiting for transfers between devices: 0.01 us -> 10.9 us  [the longest x3 7.17 us: shards(): lax.ppermute(spectrum, 'freq', [(i, i - by) for i in range(by, freq_count)])]
    all_gather x1 -> x0, blocking collectives: 10.2 us -> none  [shards(): full_plane = lax.all_gather(own_rows, 'acc', axis=0, tiled=True)]
    concatenate x9 -> x0, local copies, waits for them, and re-layouts: 9.67 us -> none  [the longest x1 9.44 us: shards(): outgoing = jnp.concatenate(slot_list, axis=1)]
  transfers between devices with their start and end apart: 2 -> 6, of which waited for: 1 -> 4; matrix products, arithmetic and copies ran while one was open for 75% -> 0% of each run, Pallas kernels for 0% -> 0%
where the time goes in v1:
time: 25.5 us; the launch traced here: 25.3 us
  waiting for transfers between devices  10.9 us (43%)
  starting transfers between devices  6.81 us (27%)
  Pallas kernels  5.12 us (20%)
  local copies, waits for them, and re-layouts  2.44 us (10%)
    ppermute x3, waiting for transfers between devices, shards(): lax.ppermute(spectrum, 'freq', [(i, i - by) for i in range(by, freq_count)])  7.17 us
    ppermute x3, starting transfers between devices, shards(): lax.ppermute(spectrum, 'freq', [(i, i - by) for i in range(by, freq_count)])  3.87 us
    ppermute x3, waiting for transfers between devices, shards(): held = held + [lax.ppermute(shard, 'acc', pairs) for shard in held]  3.71 us
    pallas_call x1, Pallas kernels, harmonic_sums(): pl.pallas_call(functools.partial(harmonic_kernel, n_slabs=len(slabs), mas...  3.33 us
    ppermute x3, starting transfers between devices, shards(): held = held + [lax.ppermute(shard, 'acc', pairs) for shard in held]  2.94 us
    unnamed x5, local copies, waits for them, and re-layouts  2.44 us
    pallas_call x1, Pallas kernels, shift_templates(): pl.pallas_call(shift_kernel, out_shape=jax.ShapeDtypeStruct((parts, round...  1.79 us
  transfers between devices with their start and end apart: 6, of which 4 were waited for; matrix products, arithmetic and copies ran while one was open for 0% of the time, Pallas kernels for 0%

profile of v1, /device:TPU:0, one launch (start us, length us, event | category | flops | bytes accessed | tf_op | source)
XLA Modules:
  0.0 25.3 jit_solution(11052178453530474064)
XLA Ops:
  0.0 1.5 %copy.4.templates_ref = bf16[2,50,384]{2,1,0:T(8,128)(2,1)} copy(bf16[2,50,384]{2,0,1:T(2,128)(2,1)} %param.4) | data formatting | bytes 153600 | tf_op args[1]
  1.5 0.0 copy-start.1
  1.5 1.8 %shift_templates.1.refs_4_ = bf16[2,64,512]{2,1,0:T(8,128)(2,1)} custom-call(s32[1,50]{1,0:T(1,128)} %bitcast.1, bf16[2,50,384]{2,1,0:T(8,128)(2,1)} %copy.4.templates_ref), custom_call_target="tpu_custom_call" | custom-call | tf_op jit(solution)/shard_map/shift_templates/pallas_call | solution.py:64
  3.3 2.9 %collective-permute-start.3 = (bf16[2,64,512]{2,1,0:T(8,128)(2,1)}, bf16[2,64,512]{2,1,0:T(8,128)(2,1)S(1)}, u32[]{:S(2)}, u32[]{:S(2)}) collective-permute-start(bf16[2,64,512]{2,1,0:T(8,128)(2,1)} %shift_templates.1.refs_4_), channel_id=1, source_target_pairs={{0,2},{1,3},{2,0},{3,1},{4,6},{5,7},{6,4},{7,5},{8,10},{9,11},{10,... | collective-permute-start | bytes 393224 | tf_op jit(solution)/shard_map/ppermute | solution.py:190
  6.3 0.0 collective-permute-start.4
  6.3 3.7 %collective-permute-done.3.refs_5_ = bf16[2,64,512]{2,1,0:T(8,128)(2,1)S(1)} collective-permute-done((bf16[2,64,512]{2,1,0:T(8,128)(2,1)}, bf16[2,64,512]{2,1,0:T(8,128)(2,1)S(1)}, u32[]{:S(2)}, u32[]{:S(2)}) %collective-permute-start.3) | collective-permute-done | bytes 131104 | tf_op jit(solution)/shard_map/ppermute | solution.py:190
  10.0 0.0 collective-permute-start.5
  10.0 0.0 copy-done.1
  10.0 1.3 %collective-permute-start.1 = (bf16[2,1024]{1,0:T(2,128)(2,1)S(1)}, bf16[2,1024]{1,0:T(2,128)(2,1)S(1)}, u32[]{:S(2)}, u32[]{:S(2)}) collective-permute-start(bf16[2,1024]{1,0:T(2,128)(2,1)S(1)} %copy-done.1), channel_id=1, source_target_pairs={{8,0},{12,4},{9,1},{13,5},{10,2},{14,6},{11,3},{15,7},{24,16},{28,... | collective-permute-start | bytes 12296 | tf_op jit(solution)/shard_map/ppermute | solution.py:184
  11.3 1.3 %collective-permute-start = (bf16[2,1024]{1,0:T(2,128)(2,1)S(1)}, bf16[2,1024]{1,0:T(2,128)(2,1)S(1)}, u32[]{:S(2)}, u32[]{:S(2)}) collective-permute-start(bf16[2,1024]{1,0:T(2,128)(2,1)S(1)} %copy-done.1), channel_id=1, source_target_pairs={{4,0},{8,4},{12,8},{5,1},{9,5},{13,9},{6,2},{10,6},{14,10},{7,3},{... | collective-permute-start | bytes 12296 | tf_op jit(solution)/shard_map/ppermute | solution.py:184
  12.6 1.3 %collective-permute-start.2 = (bf16[2,1024]{1,0:T(2,128)(2,1)S(1)}, bf16[2,1024]{1,0:T(2,128)(2,1)S(1)}, u32[]{:S(2)}, u32[]{:S(2)}) collective-permute-start(bf16[2,1024]{1,0:T(2,128)(2,1)S(1)} %copy-done.1), channel_id=1, source_target_pairs={{12,0},{13,1},{14,2},{15,3},{28,16},{29,17},{30,18},{31,19}} | collective-permute-start | bytes 12296 | tf_op jit(solution)/shard_map/ppermute | solution.py:184
  13.9 2.5 %collective-permute-done.1.refs_2_ = bf16[2,1024]{1,0:T(2,128)(2,1)S(1)} collective-permute-done((bf16[2,1024]{1,0:T(2,128)(2,1)S(1)}, bf16[2,1024]{1,0:T(2,128)(2,1)S(1)}, u32[]{:S(2)}, u32[]{:S(2)}) %collective-permute-start.1) | collective-permute-done | bytes 4128 | tf_op jit(solution)/shard_map/ppermute | solution.py:184
  16.4 0.4 %collective-permute-done.refs_1_ = bf16[2,1024]{1,0:T(2,128)(2,1)S(1)} collective-permute-done((bf16[2,1024]{1,0:T(2,128)(2,1)S(1)}, bf16[2,1024]{1,0:T(2,128)(2,1)S(1)}, u32[]{:S(2)}, u32[]{:S(2)}) %collective-permute-start) | collective-permute-done | bytes 4128 | tf_op jit(solution)/shard_map/ppermute | solution.py:184
  16.8 4.3 %collective-permute-done.2.refs_3_ = bf16[2,1024]{1,0:T(2,128)(2,1)S(1)} collective-permute-done((bf16[2,1024]{1,0:T(2,128)(2,1)S(1)}, bf16[2,1024]{1,0:T(2,128)(2,1)S(1)}, u32[]{:S(2)}, u32[]{:S(2)}) %collective-permute-start.2) | collective-permute-done | bytes 4128 | tf_op jit(solution)/shard_map/ppermute | solution.py:184
  21.0 0.0 collective-permute-done.4.refs_6_
  21.0 0.0 collective-permute-done.5.refs_7_
  21.0 0.0 copy-start
  21.0 0.9 %copy-done = bf16[2,64,512]{2,1,0:T(8,128)(2,1)S(1)} copy-done((bf16[2,64,512]{2,1,0:T(8,128)(2,1)S(1)}, bf16[2,64,512]{2,1,0:T(8,128)(2,1)}, u32[]{:S(2)}) %copy-start) | copy-done | bytes 131096
  22.0 3.3 %harmonic_sums.1 = f32[200,256]{1,0:T(8,128)} custom-call(bf16[2,1024]{1,0:T(2,128)(2,1)S(1)} %copy-done.1, bf16[2,1024]{1,0:T(2,128)(2,1)S(1)} %collective-permute-done.refs_1_, bf16[2,1024]{1,0:T(2,128)(2,1)S(1)} %collective-permute-done.1.refs_2_, bf16[2,1024]{1,0:T(2,128)(2,1)S(1)} %collective-permute-done.2.refs_3_, bf16[2,64,512]{2,1,0:T(8,128)(2,1)S(1)} %copy-done, ...), custom_call_target="tpu_custom_call" | custom-call | tf_op jit(solution)/shard_map/harmonic_sums/pallas_call | solution.py:161
Async XLA Ops:
  1.5 8.4 %copy-start.1 = (bf16[2,1024]{1,0:T(2,128)(2,1)S(1)}, bf16[2,1024]{1,0:T(2,128)(2,1)}, u32[]{:S(2)}) copy-start(bf16[2,1024]{1,0:T(2,128)(2,1)} %refs_0_.1) | copy-start | bytes 12292
  3.3 6.6 %collective-permute-start.3 = (bf16[2,64,512]{2,1,0:T(8,128)(2,1)}, bf16[2,64,512]{2,1,0:T(8,128)(2,1)S(1)}, u32[]{:S(2)}, u32[]{:S(2)}) collective-permute-start(bf16[2,64,512]{2,1,0:T(8,128)(2,1)} %shift_templates.1.refs_4_), channel_id=1, source_target_pairs={{0,2},{1,3},{2,0},{3,1},{4,6},{5,7},{6,4},{7,5},{8,10},{9,11},{10,... | collective-permute-start | bytes 393224 | tf_op jit(solution)/shard_map/ppermute | solution.py:190
  6.3 14.8 %collective-permute-start.4 = (bf16[2,64,512]{2,1,0:T(8,128)(2,1)}, bf16[2,64,512]{2,1,0:T(8,128)(2,1)S(1)}, u32[]{:S(2)}, u32[]{:S(2)}) collective-permute-start(bf16[2,64,512]{2,1,0:T(8,128)(2,1)} %shift_templates.1.refs_4_), channel_id=1, source_target_pairs={{0,1},{1,0},{2,3},{3,2},{4,5},{5,4},{6,7},{7,6},{8,9},{9,8},{10,11... | collective-permute-start | bytes 393224 | tf_op jit(solution)/shard_map/ppermute | solution.py:190
  10.0 11.1 %collective-permute-start.5 = (bf16[2,64,512]{2,1,0:T(8,128)(2,1)S(1)}, bf16[2,64,512]{2,1,0:T(8,128)(2,1)S(1)}, u32[]{:S(2)}, u32[]{:S(2)}) collective-permute-start(bf16[2,64,512]{2,1,0:T(8,128)(2,1)S(1)} %collective-permute-done.3.refs_5_), channel_id=1, source_target_pairs={{0,1},{1,0},{2,3},{3,2},{4,5},{5,4},{6,7},{7,6},{8,9},{9,8},{10,11... | collective-permute-start | bytes 393224 | tf_op jit(solution)/shard_map/ppermute | solution.py:190
  10.0 6.4 %collective-permute-start.1 = (bf16[2,1024]{1,0:T(2,128)(2,1)S(1)}, bf16[2,1024]{1,0:T(2,128)(2,1)S(1)}, u32[]{:S(2)}, u32[]{:S(2)}) collective-permute-start(bf16[2,1024]{1,0:T(2,128)(2,1)S(1)} %copy-done.1), channel_id=1, source_target_pairs={{8,0},{12,4},{9,1},{13,5},{10,2},{14,6},{11,3},{15,7},{24,16},{28,... | collective-permute-start | bytes 12296 | tf_op jit(solution)/shard_map/ppermute | solution.py:184
  11.3 5.5 %collective-permute-start = (bf16[2,1024]{1,0:T(2,128)(2,1)S(1)}, bf16[2,1024]{1,0:T(2,128)(2,1)S(1)}, u32[]{:S(2)}, u32[]{:S(2)}) collective-permute-start(bf16[2,1024]{1,0:T(2,128)(2,1)S(1)} %copy-done.1), channel_id=1, source_target_pairs={{4,0},{8,4},{12,8},{5,1},{9,5},{13,9},{6,2},{10,6},{14,10},{7,3},{... | collective-permute-start | bytes 12296 | tf_op jit(solution)/shard_map/ppermute | solution.py:184
  12.6 8.5 %collective-permute-start.2 = (bf16[2,1024]{1,0:T(2,128)(2,1)S(1)}, bf16[2,1024]{1,0:T(2,128)(2,1)S(1)}, u32[]{:S(2)}, u32[]{:S(2)}) collective-permute-start(bf16[2,1024]{1,0:T(2,128)(2,1)S(1)} %copy-done.1), channel_id=1, source_target_pairs={{12,0},{13,1},{14,2},{15,3},{28,16},{29,17},{30,18},{31,19}} | collective-permute-start | bytes 12296 | tf_op jit(solution)/shard_map/ppermute | solution.py:184
  21.0 0.9 %copy-start = (bf16[2,64,512]{2,1,0:T(8,128)(2,1)S(1)}, bf16[2,64,512]{2,1,0:T(8,128)(2,1)}, u32[]{:S(2)}) copy-start(bf16[2,64,512]{2,1,0:T(8,128)(2,1)} %shift_templates.1.refs_4_) | copy-start | bytes 393220

commit v2 on v1

v2 whole, which is shorter than its diff:
```python
import functools

import jax
import jax.numpy as jnp
from jax import lax
from jax.experimental import pallas as pl
from jax.experimental.pallas import tpu as pltpu
from jax.sharding import PartitionSpec as P

K = 384
OFF = 128
H = 8
LANES = 128
WIDTH = K + OFF
NT = (((1,), (1,)), ((), ()))
VMEM = pl.BlockSpec(memory_space=pltpu.VMEM)


def round_up(value, step):
    return (value + step - 1) // step * step


def row_blocks(rows):
    centre = rows // 2
    blocks = []
    for harmonic in range(1, H + 1):
        low = centre - centre // harmonic
        end = centre + (rows - 1 - centre) // harmonic + 1
        start = low // 16 * 16
        blocks.append((start, round_up(end, 16) - start))
    return blocks


def lane_gather(values, index):
    return jnp.take_along_axis(values, index, axis=1, mode="promise_in_bounds")


def pick_kernel(*refs, masks, shard_rows, rows):
    held = refs[: len(masks)]
    picked, taps = refs[len(masks) :]
    acc_index = lax.axis_index("acc")
    both = 2 * shard_rows
    padded = taps.shape[0] // len(masks)
    tap_tiles = held[0].shape[2] // LANES
    lane = lax.broadcasted_iota(jnp.int32, (padded, LANES), 1)
    spot = lax.broadcasted_iota(jnp.int32, (padded, shard_rows), 0) // 2 == lax.broadcasted_iota(
        jnp.int32, (padded, shard_rows), 1
    )
    for slot in range(len(masks)):
        values = held[slot][...].reshape(both + 2, held[slot].shape[2]).astype(jnp.float32)
        packed = values[both : both + 1, :shard_rows]
        values = values[:both]
        values = jnp.concatenate([values, jnp.zeros((padded - both, values.shape[1]), jnp.float32)], axis=0)
        offset = jnp.sum(jnp.where(spot, packed, 0.0), axis=1, keepdims=True)
        offset = jnp.broadcast_to(offset.astype(jnp.int32), (padded, LANES))
        index = (lane - offset) & (LANES - 1)
        stays = lane >= offset
        before = jnp.zeros((padded, LANES), jnp.float32)
        for tile in range(tap_tiles + 1):
            if tile < tap_tiles:
                turned = lane_gather(values[:, tile * LANES : (tile + 1) * LANES], index)
            else:
                turned = jnp.zeros((padded, LANES), jnp.float32)
            placed = jnp.where(stays, turned, before).astype(jnp.bfloat16)
            taps[slot * padded : (slot + 1) * padded, tile * LANES : (tile + 1) * LANES] = placed
            before = turned

    centre = rows // 2
    column = lax.broadcasted_iota(jnp.int32, (1, taps.shape[0]), 1)
    row_at = jnp.full(column.shape, -2 * H * rows, jnp.int32)
    for slot, mask in enumerate(masks):
        inside = (column >= slot * padded) & (column < slot * padded + both)
        row_at = jnp.where(inside, (acc_index ^ mask) * both + column - slot * padded, row_at)
    at = 0
    for harmonic, (start, count) in enumerate(row_blocks(rows), 1):
        row = lax.broadcasted_iota(jnp.int32, (count, taps.shape[0]), 0) + start
        wanted = 2 * (centre + harmonic * (row - centre))
        for part in range(2):
            choose = jnp.where(wanted + part == row_at, 1.0, 0.0).astype(jnp.bfloat16)
            chosen = jnp.dot(choose, taps[...], preferred_element_type=jnp.float32)
            picked[at : at + count, :] = chosen.astype(jnp.bfloat16)
            at += count


def pick_templates(held, masks, rows):
    shard_rows = held[0].shape[0] - 1
    picked_rows = 2 * sum(count for _, count in row_blocks(rows))
    return pl.pallas_call(
        functools.partial(pick_kernel, masks=masks, shard_rows=shard_rows, rows=rows),
        out_shape=jax.ShapeDtypeStruct((picked_rows, WIDTH), jnp.bfloat16),
        in_specs=[VMEM] * len(masks),
        out_specs=VMEM,
        scratch_shapes=[pltpu.VMEM((len(masks) * round_up(2 * shard_rows, 16), WIDTH), jnp.bfloat16)],
        compiler_params=pltpu.CompilerParams(vmem_limit_bytes=16 << 20),
        name="pick_templates",
    )(*held)


def harmonic_kernel(*refs, n_slabs, rows):
    slabs = refs[:n_slabs]
    picked, out_ref, line, windows, total = refs[n_slabs:]
    sub_bins = out_ref.shape[1]
    blocks_f = sub_bins // LANES
    window_tiles = WIDTH // LANES
    slab_tiles = slabs[0].shape[1] // LANES
    filled = n_slabs * slab_tiles
    freq_index = lax.axis_index("freq")
    acc_index = lax.axis_index("acc")
    blocks = row_blocks(rows)

    line[:, filled:, :] = jnp.zeros((2, line.shape[1] - filled, LANES), jnp.float32)
    for slot, slab in enumerate(slabs[::-1]):
        values = slab[...].astype(jnp.float32)
        for tile in range(slab_tiles):
            for part in range(2):
                line[part, pl.ds(slot * slab_tiles + tile, 1), :] = values[part : part + 1, tile * LANES : (tile + 1) * LANES]

    lane = lax.broadcasted_iota(jnp.int32, (16, LANES), 1)
    sublane = lax.broadcasted_iota(jnp.int32, (16, LANES), 0)
    total[...] = jnp.zeros_like(total)
    at = 0
    for harmonic in range(1, H + 1):
        place = lane + harmonic * sublane
        index = place & (LANES - 1)
        stays = place < LANES
        n_tiles = window_tiles + harmonic * blocks_f
        first = ((harmonic - 1) * freq_index * slab_tiles) + harmonic * acc_index * blocks_f
        first = jnp.minimum(first, filled)
        for part in range(2):
            turned = []
            for tile in range(n_tiles + 1):
                values = jnp.broadcast_to(line[part, pl.ds(first + tile, 1), :], (16, LANES))
                turned.append(lane_gather(values, index))
            base = [jnp.where(stays, turned[t], turned[t + 1]).astype(jnp.bfloat16) for t in range(n_tiles)]
            moved = {0: base}
            for group in range(LANES // 16):
                tile_by, lane_by = divmod(16 * harmonic * group, LANES)
                if lane_by not in moved:
                    rolled = [pltpu.roll(values, LANES - lane_by, 1) for values in base]
                    keep = lane < LANES - lane_by
                    moved[lane_by] = [jnp.where(keep, rolled[t], rolled[min(t + 1, n_tiles - 1)]) for t in range(n_tiles)]
                for block in range(blocks_f):
                    for tile in range(window_tiles):
                        row = block * LANES + 16 * group
                        windows[harmonic - 1, part, row : row + 16, tile * LANES : (tile + 1) * LANES] = moved[lane_by][
                            tile_by + harmonic * block + tile
                        ]
        start, count = blocks[harmonic - 1]
        chosen = picked[at : at + 2 * count, :]
        at += 2 * count
        with_real = lax.dot_general(chosen, windows[harmonic - 1, 0], NT, preferred_element_type=jnp.float32)
        with_imag = lax.dot_general(chosen, windows[harmonic - 1, 1], NT, preferred_element_type=jnp.float32)
        real = with_real[:count] - with_imag[count:]
        imag = with_imag[:count] + with_real[count:]
        power = (real * real + imag * imag).astype(jnp.bfloat16)
        total[start : start + count, :] += power.astype(jnp.float32)
    out_ref[...] = total[:rows, :]


def harmonic_sums(slabs, picked, rows, sub_bins):
    filled = len(slabs) * slabs[0].shape[1] // LANES
    beyond = WIDTH // LANES + H * (sub_bins // LANES) + 1
    return pl.pallas_call(
        functools.partial(harmonic_kernel, n_slabs=len(slabs), rows=rows),
        out_shape=jax.ShapeDtypeStruct((rows, sub_bins), jnp.float32),
        in_specs=[VMEM] * (len(slabs) + 1),
        out_specs=VMEM,
        scratch_shapes=[
            pltpu.VMEM((2, filled + beyond, LANES), jnp.float32),
            pltpu.VMEM((H, 2, sub_bins, WIDTH), jnp.bfloat16),
            pltpu.VMEM((round_up(rows, 16), sub_bins), jnp.float32),
        ],
        compiler_params=pltpu.CompilerParams(vmem_limit_bytes=32 << 20),
        name="harmonic_sums",
    )(*slabs, picked)


def exchanged(values, step):
    count = lax.axis_size("acc")
    return [lax.ppermute(value, "acc", [(i, i ^ step) for i in range(count)]) for value in values]


def shards(spectrum, templates, offsets):
    freq_count = lax.axis_size("freq")
    acc_count = lax.axis_size("acc")
    held = jnp.transpose(templates, (1, 0, 2))
    rows = acc_count * held.shape[0]
    extra = jnp.pad(offsets.astype(jnp.bfloat16), (0, held.shape[2] - offsets.shape[0]))
    held = [jnp.concatenate([held, jnp.broadcast_to(extra, (1,) + held.shape[1:])], axis=0)]
    slabs = [
        lax.ppermute(spectrum, "freq", [(i, i - by) for i in range(by, freq_count)]) for by in range(freq_count - 1, 0, -1)
    ] + [spectrum]
    masks = list(range(acc_count))
    for mask in masks[:0:-1]:
        held = held[:1] + exchanged(held[:1], mask) + held[1:]
    picked = pick_templates(held, masks, rows)
    return harmonic_sums(slabs, picked, rows, spectrum.shape[1] // acc_count)


def solution(mesh):
    return jax.shard_map(
        shards,
        mesh=mesh,
        in_specs=(P(None, ("trial", "freq")), P(None, "acc", None), P("acc")),
        out_specs=P(None, ("trial", "freq", "acc")),
        check_vma=False,
    )
```

time: 25.5 us -> 16.6 us (0.65)
  waiting for transfers between devices: 10.9 us -> 2.44 us
  local copies, waits for them, and re-layouts: 2.44 us -> 0.02 us
  other arithmetic: 0 us -> 1.67 us
    ppermute x3, waiting for transfers between devices: 7.17 us -> 2.09 us  [shards(): lax.ppermute(spectrum, 'freq', [(i, i - by) for i in range(by, freq_count)])]
    ppermute x3, waiting for transfers between devices: 3.71 us -> 0.35 us  [exchanged(): lax.ppermute(value, 'acc', [(i, i ^ step) for i in range(count)])]
    unnamed x5 -> x2, local copies, waits for them, and re-layouts: 2.44 us -> 0.01 us
    concatenate x0 -> x1, other arithmetic: none -> 1 us  [shards(): jnp.concatenate([held, jnp.broadcast_to(extra, (1,) + held.shape[1:])], a...]
    convert_element_type x0 -> x1, other arithmetic: none -> 0.67 us  [shards(): offsets.astype(jnp.bfloat16)]
  transfers between devices with their start and end apart: 6 -> 6, of which waited for: 4 -> 4; matrix products, arithmetic and copies ran while one was open for 0% -> 0% of each run, Pallas kernels for 0% -> 12%
where the time goes in v2:
time: 16.6 us; the launch traced here: 16.3 us
  starting transfers between devices  7.02 us (42%)
  Pallas kernels  5.15 us (31%)
  waiting for transfers between devices  2.44 us (15%)
  other arithmetic  1.67 us (10%)
    ppermute x3, starting transfers between devices, shards(): lax.ppermute(spectrum, 'freq', [(i, i - by) for i in range(by, freq_count)])  3.86 us
    pallas_call x1, Pallas kernels, harmonic_sums(): pl.pallas_call(functools.partial(harmonic_kernel, n_slabs=len(slabs), row...  3.19 us
    ppermute x3, starting transfers between devices, exchanged(): lax.ppermute(value, 'acc', [(i, i ^ step) for i in range(count)])  3.15 us
    ppermute x3, waiting for transfers between devices, shards(): lax.ppermute(spectrum, 'freq', [(i, i - by) for i in range(by, freq_count)])  2.09 us
    pallas_call x1, Pallas kernels, pick_templates(): pl.pallas_call(functools.partial(pick_kernel, masks=masks, shard_rows=sha...  1.96 us
    concatenate x1, other arithmetic, shards(): jnp.concatenate([held, jnp.broadcast_to(extra, (1,) + held.shape[1:])], a...  1 us
    convert_element_type x1, other arithmetic, shards(): offsets.astype(jnp.bfloat16)  0.67 us
    ppermute x3, waiting for transfers between devices, exchanged(): lax.ppermute(value, 'acc', [(i, i ^ step) for i in range(count)])  0.35 us
  transfers between devices with their start and end apart: 6, of which 4 were waited for; matrix products, arithmetic and copies ran while one was open for 0% of the time, Pallas kernels for 12%

profile of v2, /device:TPU:0, one launch (start us, length us, event | category | flops | bytes accessed | tf_op | source)
XLA Modules:
  0.0 16.3 jit_solution(3731259138518001263)
XLA Ops:
  0.0 0.0 copy-start
  0.0 0.7 %convert_element_type.5 = bf16[50]{0:T(256)(128)(2,1)S(1)} convert(s32[50]{0:T(128)} %param.5) | non-fusion elementwise | flops 50 | bytes 300 | tf_op jit(solution)/shard_map/convert_element_type | solution.py:188
  0.7 1.0 %pad_maximum_fusion.refs_0_ = bf16[51,2,384]{2,1,0:T(2,128)(2,1)S(1)} fusion(bf16[1,2,384]{2,1,0:T(2,128)(2,1)S(1)} %broadcast_in_dim.3, bf16[50,2,384]{2,1,0:T(2,128)(2,1)} %bitcast.1), kind=kLoop, calls=%fused_computation | loop fusion | flops 39168 | bytes 156672 | tf_op jit(solution)/shard_map/concatenate | solution.py:189
  1.7 0.5 %collective-permute-start.3 = (bf16[51,2,384]{2,1,0:T(2,128)(2,1)S(1)}, bf16[51,2,384]{2,1,0:T(2,128)(2,1)S(1)}, u32[]{:S(2)}, u32[]{:S(2)}) collective-permute-start(bf16[51,2,384]{2,1,0:T(2,128)(2,1)S(1)} %pad_maximum_fusion.refs_0_), channel_id=1, source_target_pairs={{0,1},{1,0},{2,3},{3,2},{4,5},{5,4},{6,7},{7,6},{8,9},{9,8},{10,11... | collective-permute-start | bytes 235016 | tf_op jit(solution)/shard_map/ppermute | solution.py:180
  2.2 2.6 %collective-permute-start.4 = (bf16[51,2,384]{2,1,0:T(2,128)(2,1)S(1)}, bf16[51,2,384]{2,1,0:T(2,128)(2,1)S(1)}, u32[]{:S(2)}, u32[]{:S(2)}) collective-permute-start(bf16[51,2,384]{2,1,0:T(2,128)(2,1)S(1)} %pad_maximum_fusion.refs_0_), channel_id=1, source_target_pairs={{0,2},{1,3},{2,0},{3,1},{4,6},{5,7},{6,4},{7,5},{8,10},{9,11},{10,... | collective-permute-start | bytes 235016 | tf_op jit(solution)/shard_map/ppermute | solution.py:180
  4.8 0.1 collective-permute-start.5
  4.8 1.3 %collective-permute-start = (bf16[2,1024]{1,0:T(2,128)(2,1)}, bf16[2,1024]{1,0:T(2,128)(2,1)S(1)}, u32[]{:S(2)}, u32[]{:S(2)}) collective-permute-start(bf16[2,1024]{1,0:T(2,128)(2,1)} %refs_3_.1), channel_id=1, source_target_pairs={{12,0},{13,1},{14,2},{15,3},{28,16},{29,17},{30,18},{31,19}} | collective-permute-start | bytes 12296 | tf_op jit(solution)/shard_map/ppermute | solution.py:191
  6.1 1.3 %collective-permute-start.1 = (bf16[2,1024]{1,0:T(2,128)(2,1)}, bf16[2,1024]{1,0:T(2,128)(2,1)S(1)}, u32[]{:S(2)}, u32[]{:S(2)}) collective-permute-start(bf16[2,1024]{1,0:T(2,128)(2,1)} %refs_3_.1), channel_id=1, source_target_pairs={{8,0},{12,4},{9,1},{13,5},{10,2},{14,6},{11,3},{15,7},{24,16},{28,... | collective-permute-start | bytes 12296 | tf_op jit(solution)/shard_map/ppermute | solution.py:191
  7.4 0.0 collective-permute-done.3.refs_1_
  7.4 1.3 %collective-permute-start.2 = (bf16[2,1024]{1,0:T(2,128)(2,1)}, bf16[2,1024]{1,0:T(2,128)(2,1)S(1)}, u32[]{:S(2)}, u32[]{:S(2)}) collective-permute-start(bf16[2,1024]{1,0:T(2,128)(2,1)} %refs_3_.1), channel_id=1, source_target_pairs={{4,0},{8,4},{12,8},{5,1},{9,5},{13,9},{6,2},{10,6},{14,10},{7,3},{... | collective-permute-start | bytes 12296 | tf_op jit(solution)/shard_map/ppermute | solution.py:191
  8.7 0.0 collective-permute-done.4.refs_2_
  8.8 0.3 %collective-permute-done.5.refs_3_ = bf16[51,2,384]{2,1,0:T(2,128)(2,1)S(1)} collective-permute-done((bf16[51,2,384]{2,1,0:T(2,128)(2,1)S(1)}, bf16[51,2,384]{2,1,0:T(2,128)(2,1)S(1)}, u32[]{:S(2)}, u32[]{:S(2)}) %collective-permute-start.5) | collective-permute-done | bytes 78368 | tf_op jit(solution)/shard_map/ppermute | solution.py:180
  9.1 2.0 %pick_templates.1.refs_4_ = bf16[1312,512]{1,0:T(8,128)(2,1)S(1)} custom-call(bf16[51,2,384]{2,1,0:T(2,128)(2,1)S(1)} %pad_maximum_fusion.refs_0_, bf16[51,2,384]{2,1,0:T(2,128)(2,1)S(1)} %collective-permute-done.3.refs_1_, bf16[51,2,384]{2,1,0:T(2,128)(2,1)S(1)} %collective-permute-done.4.refs_2_, bf16[51,2,384]{2,1,0:T(2,128)(2,1)S(1)} %collective-permute-done.5.refs_3_), custom_call_target="tpu_custom_call" | custom-call | tf_op jit(solution)/shard_map/pick_templates/pallas_call | solution.py:88
  11.1 1.3 %collective-permute-done.refs_0_ = bf16[2,1024]{1,0:T(2,128)(2,1)S(1)} collective-permute-done((bf16[2,1024]{1,0:T(2,128)(2,1)}, bf16[2,1024]{1,0:T(2,128)(2,1)S(1)}, u32[]{:S(2)}, u32[]{:S(2)}) %collective-permute-start) | collective-permute-done | bytes 4128 | tf_op jit(solution)/shard_map/ppermute | solution.py:191
  12.4 0.4 %collective-permute-done.1.refs_1_ = bf16[2,1024]{1,0:T(2,128)(2,1)S(1)} collective-permute-done((bf16[2,1024]{1,0:T(2,128)(2,1)}, bf16[2,1024]{1,0:T(2,128)(2,1)S(1)}, u32[]{:S(2)}, u32[]{:S(2)}) %collective-permute-start.1) | collective-permute-done | bytes 4128 | tf_op jit(solution)/shard_map/ppermute | solution.py:191
  12.7 0.4 %collective-permute-done.2.refs_2_ = bf16[2,1024]{1,0:T(2,128)(2,1)S(1)} collective-permute-done((bf16[2,1024]{1,0:T(2,128)(2,1)}, bf16[2,1024]{1,0:T(2,128)(2,1)S(1)}, u32[]{:S(2)}, u32[]{:S(2)}) %collective-permute-start.2) | collective-permute-done | bytes 4128 | tf_op jit(solution)/shard_map/ppermute | solution.py:191
  13.2 0.0 copy-done
  13.2 3.2 %harmonic_sums.1 = f32[200,256]{1,0:T(8,128)} custom-call(bf16[2,1024]{1,0:T(2,128)(2,1)S(1)} %collective-permute-done.refs_0_, bf16[2,1024]{1,0:T(2,128)(2,1)S(1)} %collective-permute-done.1.refs_1_, bf16[2,1024]{1,0:T(2,128)(2,1)S(1)} %collective-permute-done.2.refs_2_, bf16[2,1024]{1,0:T(2,128)(2,1)S(1)} %copy-done, ...), custom_call_target="tpu_custom_call" | custom-call | tf_op jit(solution)/shard_map/harmonic_sums/pallas_call | solution.py:163
  (2 shorter events, 0.0 us)
Async XLA Ops:
  0.0 13.2 %copy-start = (bf16[2,1024]{1,0:T(2,128)(2,1)S(1)}, bf16[2,1024]{1,0:T(2,128)(2,1)}, u32[]{:S(2)}) copy-start(bf16[2,1024]{1,0:T(2,128)(2,1)} %refs_3_.1) | copy-start | bytes 12292
  1.7 5.7 %collective-permute-start.3 = (bf16[51,2,384]{2,1,0:T(2,128)(2,1)S(1)}, bf16[51,2,384]{2,1,0:T(2,128)(2,1)S(1)}, u32[]{:S(2)}, u32[]{:S(2)}) collective-permute-start(bf16[51,2,384]{2,1,0:T(2,128)(2,1)S(1)} %pad_maximum_fusion.refs_0_), channel_id=1, source_target_pairs={{0,1},{1,0},{2,3},{3,2},{4,5},{5,4},{6,7},{7,6},{8,9},{9,8},{10,11... | collective-permute-start | bytes 235016 | tf_op jit(solution)/shard_map/ppermute | solution.py:180
  2.2 6.5 %collective-permute-start.4 = (bf16[51,2,384]{2,1,0:T(2,128)(2,1)S(1)}, bf16[51,2,384]{2,1,0:T(2,128)(2,1)S(1)}, u32[]{:S(2)}, u32[]{:S(2)}) collective-permute-start(bf16[51,2,384]{2,1,0:T(2,128)(2,1)S(1)} %pad_maximum_fusion.refs_0_), channel_id=1, source_target_pairs={{0,2},{1,3},{2,0},{3,1},{4,6},{5,7},{6,4},{7,5},{8,10},{9,11},{10,... | collective-permute-start | bytes 235016 | tf_op jit(solution)/shard_map/ppermute | solution.py:180
  4.8 4.3 %collective-permute-start.5 = (bf16[51,2,384]{2,1,0:T(2,128)(2,1)S(1)}, bf16[51,2,384]{2,1,0:T(2,128)(2,1)S(1)}, u32[]{:S(2)}, u32[]{:S(2)}) collective-permute-start(bf16[51,2,384]{2,1,0:T(2,128)(2,1)S(1)} %pad_maximum_fusion.refs_0_), channel_id=1, source_target_pairs={{0,3},{1,2},{2,1},{3,0},{4,7},{5,6},{6,5},{7,4},{8,11},{9,10},{10,... | collective-permute-start | bytes 235016 | tf_op jit(solution)/shard_map/ppermute | solution.py:180
  4.8 7.5 %collective-permute-start = (bf16[2,1024]{1,0:T(2,128)(2,1)}, bf16[2,1024]{1,0:T(2,128)(2,1)S(1)}, u32[]{:S(2)}, u32[]{:S(2)}) collective-permute-start(bf16[2,1024]{1,0:T(2,128)(2,1)} %refs_3_.1), channel_id=1, source_target_pairs={{12,0},{13,1},{14,2},{15,3},{28,16},{29,17},{30,18},{31,19}} | collective-permute-start | bytes 12296 | tf_op jit(solution)/shard_map/ppermute | solution.py:191
  6.1 6.6 %collective-permute-start.1 = (bf16[2,1024]{1,0:T(2,128)(2,1)}, bf16[2,1024]{1,0:T(2,128)(2,1)S(1)}, u32[]{:S(2)}, u32[]{:S(2)}) collective-permute-start(bf16[2,1024]{1,0:T(2,128)(2,1)} %refs_3_.1), channel_id=1, source_target_pairs={{8,0},{12,4},{9,1},{13,5},{10,2},{14,6},{11,3},{15,7},{24,16},{28,... | collective-permute-start | bytes 12296 | tf_op jit(solution)/shard_map/ppermute | solution.py:191
  7.4 5.7 %collective-permute-start.2 = (bf16[2,1024]{1,0:T(2,128)(2,1)}, bf16[2,1024]{1,0:T(2,128)(2,1)S(1)}, u32[]{:S(2)}, u32[]{:S(2)}) collective-permute-start(bf16[2,1024]{1,0:T(2,128)(2,1)} %refs_3_.1), channel_id=1, source_target_pairs={{4,0},{8,4},{12,8},{5,1},{9,5},{13,9},{6,2},{10,6},{14,10},{7,3},{... | collective-permute-start | bytes 12296 | tf_op jit(solution)/shard_map/ppermute | solution.py:191

commit v3 on v2

--- a/solution.py
+++ b/solution.py
@@ -35,50 +35,60 @@
     return jnp.take_along_axis(values, index, axis=1, mode="promise_in_bounds")
 
 
+def pack_templates(templates, offsets):
+    rows, parts, taps = templates.shape
+    wide = jnp.broadcast_to(jnp.pad(offsets, (0, taps - rows)), (1, parts, taps))
+    return jnp.concatenate([templates, wide.astype(templates.dtype)], axis=0)
+
+
+def pick_margins(rows):
+    centre = rows // 2
+    reach = [
+        (centre + harmonic * (start - centre), centre + harmonic * (start + count - 1 - centre))
+        for harmonic, (start, count) in enumerate(row_blocks(rows), 1)
+    ]
+    return round_up(max(0, -min(low for low, _ in reach)), 8), round_up(max(0, max(high for _, high in reach) + 1 - rows), 8)
+
+
 def pick_kernel(*refs, masks, shard_rows, rows):
     held = refs[: len(masks)]
     picked, taps = refs[len(masks) :]
     acc_index = lax.axis_index("acc")
-    both = 2 * shard_rows
-    padded = taps.shape[0] // len(masks)
     tap_tiles = held[0].shape[2] // LANES
-    lane = lax.broadcasted_iota(jnp.int32, (padded, LANES), 1)
-    spot = lax.broadcasted_iota(jnp.int32, (padded, shard_rows), 0) // 2 == lax.broadcasted_iota(
-        jnp.int32, (padded, shard_rows), 1
+    tiles = tap_tiles + 1
+    before_rows, after_rows = pick_margins(rows)
+    lane = lax.broadcasted_iota(jnp.int32, (shard_rows, LANES), 1)
+    spot = lax.broadcasted_iota(jnp.int32, (shard_rows, shard_rows), 0) == lax.broadcasted_iota(
+        jnp.int32, (shard_rows, shard_rows), 1
     )
-    for slot in range(len(masks)):
-        values = held[slot][...].reshape(both + 2, held[slot].shape[2]).astype(jnp.float32)
-        packed = values[both : both + 1, :shard_rows]
-        values = values[:both]
-        values = jnp.concatenate([values, jnp.zeros((padded - both, values.shape[1]), jnp.float32)], axis=0)
+    taps[:, :before_rows, :] = jnp.zeros((2 * tiles, before_rows, LANES), jnp.float32)
+    taps[:, before_rows + rows :, :] = jnp.zeros((2 * tiles, taps.shape[1] - before_rows - rows, LANES), jnp.float32)
+    for slot, mask in enumerate(masks):
+        packed = held[slot][shard_rows, 0:1, :shard_rows].astype(jnp.float32)
         offset = jnp.sum(jnp.where(spot, packed, 0.0), axis=1, keepdims=True)
-        offset = jnp.broadcast_to(offset.astype(jnp.int32), (padded, LANES))
+        offset = jnp.broadcast_to(offset.astype(jnp.int32), (shard_rows, LANES))
         index = (lane - offset) & (LANES - 1)
         stays = lane >= offset
-        before = jnp.zeros((padded, LANES), jnp.float32)
-        for tile in range(tap_tiles + 1):
-            if tile < tap_tiles:
-                turned = lane_gather(values[:, tile * LANES : (tile + 1) * LANES], index)
-            else:
-                turned = jnp.zeros((padded, LANES), jnp.float32)
-            placed = jnp.where(stays, turned, before).astype(jnp.bfloat16)
-            taps[slot * padded : (slot + 1) * padded, tile * LANES : (tile + 1) * LANES] = placed
-            before = turned
+        first_row = before_rows + (acc_index ^ mask) * shard_rows
+        for part in range(2):
+            values = held[slot][:shard_rows, part, :].astype(jnp.float32)
+            before = jnp.zeros((shard_rows, LANES), jnp.float32)
+            for tile in range(tiles):
+                if tile < tap_tiles:
+                    turned = lane_gather(values[:, tile * LANES : (tile + 1) * LANES], index)
+                else:
+                    turned = jnp.zeros((shard_rows, LANES), jnp.float32)
+                taps[part * tiles + tile, pl.ds(first_row, shard_rows), :] = jnp.where(stays, turned, before)
+                before = turned
 
     centre = rows // 2
-    column = lax.broadcasted_iota(jnp.int32, (1, taps.shape[0]), 1)
-    row_at = jnp.full(column.shape, -2 * H * rows, jnp.int32)
-    for slot, mask in enumerate(masks):
-        inside = (column >= slot * padded) & (column < slot * padded + both)
-        row_at = jnp.where(inside, (acc_index ^ mask) * both + column - slot * padded, row_at)
     at = 0
     for harmonic, (start, count) in enumerate(row_blocks(rows), 1):
-        row = lax.broadcasted_iota(jnp.int32, (count, taps.shape[0]), 0) + start
-        wanted = 2 * (centre + harmonic * (row - centre))
+        first_row = before_rows + centre + harmonic * (start - centre)
         for part in range(2):
-            choose = jnp.where(wanted + part == row_at, 1.0, 0.0).astype(jnp.bfloat16)
-            chosen = jnp.dot(choose, taps[...], preferred_element_type=jnp.float32)
-            picked[at : at + count, :] = chosen.astype(jnp.bfloat16)
+            for tile in range(tiles):
+                chosen = taps[part * tiles + tile, pl.ds(first_row, count, stride=harmonic), :]
+                picked[at : at + count, tile * LANES : (tile + 1) * LANES] = chosen.astype(jnp.bfloat16)
             at += count
 
 
@@ -90,7 +100,7 @@
         out_shape=jax.ShapeDtypeStruct((picked_rows, WIDTH), jnp.bfloat16),
         in_specs=[VMEM] * len(masks),
         out_specs=VMEM,
-        scratch_shapes=[pltpu.VMEM((len(masks) * round_up(2 * shard_rows, 16), WIDTH), jnp.bfloat16)],
+        scratch_shapes=[pltpu.VMEM((2 * WIDTH // LANES, rows + sum(pick_margins(rows)), LANES), jnp.float32)],
         compiler_params=pltpu.CompilerParams(vmem_limit_bytes=16 << 20),
         name="pick_templates",
     )(*held)
@@ -109,11 +119,12 @@
     blocks = row_blocks(rows)
 
     line[:, filled:, :] = jnp.zeros((2, line.shape[1] - filled, LANES), jnp.float32)
-    for slot, slab in enumerate(slabs[::-1]):
+    for mask, slab in zip(range(n_slabs - 1, -1, -1), slabs):
         values = slab[...].astype(jnp.float32)
+        place = (freq_index ^ mask) * slab_tiles
         for tile in range(slab_tiles):
             for part in range(2):
-                line[part, pl.ds(slot * slab_tiles + tile, 1), :] = values[part : part + 1, tile * LANES : (tile + 1) * LANES]
+                line[part, pl.ds(place + tile, 1), :] = values[part : part + 1, tile * LANES : (tile + 1) * LANES]
 
     lane = lax.broadcasted_iota(jnp.int32, (16, LANES), 1)
     sublane = lax.broadcasted_iota(jnp.int32, (16, LANES), 0)
@@ -124,8 +135,7 @@
         index = place & (LANES - 1)
         stays = place < LANES
         n_tiles = window_tiles + harmonic * blocks_f
-        first = ((harmonic - 1) * freq_index * slab_tiles) + harmonic * acc_index * blocks_f
-        first = jnp.minimum(first, filled)
+        first = jnp.minimum(harmonic * (freq_index * slab_tiles + acc_index * blocks_f), filled)
         for part in range(2):
             turned = []
             for tile in range(n_tiles + 1):
@@ -175,25 +185,18 @@
     )(*slabs, picked)
 
 
-def exchanged(values, step):
-    count = lax.axis_size("acc")
-    return [lax.ppermute(value, "acc", [(i, i ^ step) for i in range(count)]) for value in values]
+def exchanged(value, axis):
+    count = lax.axis_size(axis)
+    masks = range(count - 1, 0, -1)
+    return [lax.ppermute(value, axis, [(i, i ^ mask) for i in range(count)]) for mask in masks] + [value]
 
 
 def shards(spectrum, templates, offsets):
-    freq_count = lax.axis_size("freq")
     acc_count = lax.axis_size("acc")
-    held = jnp.transpose(templates, (1, 0, 2))
-    rows = acc_count * held.shape[0]
-    extra = jnp.pad(offsets.astype(jnp.bfloat16), (0, held.shape[2] - offsets.shape[0]))
-    held = [jnp.concatenate([held, jnp.broadcast_to(extra, (1,) + held.shape[1:])], axis=0)]
-    slabs = [
-        lax.ppermute(spectrum, "freq", [(i, i - by) for i in range(by, freq_count)]) for by in range(freq_count - 1, 0, -1)
-    ] + [spectrum]
-    masks = list(range(acc_count))
-    for mask in masks[:0:-1]:
-        held = held[:1] + exchanged(held[:1], mask) + held[1:]
-    picked = pick_templates(held, masks, rows)
+    rows = acc_count * templates.shape[1]
+    slabs = exchanged(spectrum, "freq")
+    held = exchanged(pack_templates(jnp.transpose(templates, (1, 0, 2)), offsets), "acc")[::-1]
+    picked = pick_templates(held, range(acc_count), rows)
     return harmonic_sums(slabs, picked, rows, spectrum.shape[1] // acc_count)
 
 

time: 16.6 us -> 16.8 us (1.012)
  Pallas kernels: 5.15 us -> 4.45 us
  starting transfers between devices: 7.02 us -> 7.56 us
  waiting for transfers between devices: 2.44 us -> 2.89 us
    pallas_call x1, Pallas kernels: 1.96 us -> 1.24 us  [pick_templates(): pl.pallas_call(functools.partial(pick_kernel, masks=masks, shard_rows=sha...]
    another operation x0 -> x1, other arithmetic: none -> 0.67 us
    convert_element_type x1 -> x0, other arithmetic: 0.67 us -> none  [shards(): offsets.astype(jnp.bfloat16)]
    ppermute x6, starting transfers between devices: 7.02 us -> 7.56 us  [exchanged(): lax.ppermute(value, axis, [(i, i ^ mask) for i in range(count)])]
    ppermute x6, waiting for transfers between devices: 2.44 us -> 2.89 us  [exchanged(): lax.ppermute(value, axis, [(i, i ^ mask) for i in range(count)])]
  transfers between devices with their start and end apart: 6 -> 6, of which waited for: 4 -> 1; matrix products, arithmetic and copies ran while one was open for 0% -> 0% of each run, Pallas kernels for 12% -> 7%
where the time goes in v3:
time: 16.8 us; the launch traced here: 16.6 us
  starting transfers between devices  7.56 us (45%)
  Pallas kernels  4.45 us (26%)
  waiting for transfers between devices  2.89 us (17%)
  other arithmetic  1.67 us (10%)
    ppermute x6, starting transfers between devices, exchanged(): lax.ppermute(value, axis, [(i, i ^ mask) for i in range(count)])  7.56 us
    pallas_call x1, Pallas kernels, harmonic_sums(): pl.pallas_call(functools.partial(harmonic_kernel, n_slabs=len(slabs), row...  3.2 us
    ppermute x6, waiting for transfers between devices, exchanged(): lax.ppermute(value, axis, [(i, i ^ mask) for i in range(count)])  2.89 us
    pallas_call x1, Pallas kernels, pick_templates(): pl.pallas_call(functools.partial(pick_kernel, masks=masks, shard_rows=sha...  1.24 us
    concatenate x1, other arithmetic, pack_templates(): return jnp.concatenate([templates, wide.astype(templates.dtype)], axis=0)  1 us
    another operation x1, other arithmetic  0.67 us
  transfers between devices with their start and end apart: 6, of which 1 were waited for; matrix products, arithmetic and copies ran while one was open for 0% of the time, Pallas kernels for 7%

profile of v3, /device:TPU:0, one launch (start us, length us, event | category | flops | bytes accessed | tf_op | source)
XLA Modules:
  0.0 16.6 jit_solution(1953678699522379543)
XLA Ops:
  0.0 0.0 copy-start
  0.0 0.7 %convert.4 = bf16[50]{0:T(256)(128)(2,1)S(1)} convert(s32[50]{0:T(128)} %param.5) | non-fusion elementwise | flops 50 | bytes 300 | tf_op jit(solution)/shard_map/convert
  0.7 1.0 %pad_maximum_fusion.refs_0_ = bf16[51,2,384]{2,1,0:T(2,128)(2,1)S(1)} fusion(bf16[1,2,384]{2,1,0:T(2,128)(2,1)S(1)} %broadcast_in_dim.3, bf16[50,2,384]{2,1,0:T(2,128)(2,1)} %bitcast.1), kind=kLoop, calls=%fused_computation | loop fusion | flops 39168 | bytes 156672 | tf_op jit(solution)/shard_map/concatenate | solution.py:41
  1.7 0.5 %collective-permute-start.3 = (bf16[51,2,384]{2,1,0:T(2,128)(2,1)S(1)}, bf16[51,2,384]{2,1,0:T(2,128)(2,1)S(1)}, u32[]{:S(2)}, u32[]{:S(2)}) collective-permute-start(bf16[51,2,384]{2,1,0:T(2,128)(2,1)S(1)} %pad_maximum_fusion.refs_0_), channel_id=1, source_target_pairs={{0,1},{1,0},{2,3},{3,2},{4,5},{5,4},{6,7},{7,6},{8,9},{9,8},{10,11... | collective-permute-start | bytes 235016 | tf_op jit(solution)/shard_map/ppermute | solution.py:191
  2.2 2.6 %collective-permute-start.4 = (bf16[51,2,384]{2,1,0:T(2,128)(2,1)S(1)}, bf16[51,2,384]{2,1,0:T(2,128)(2,1)S(1)}, u32[]{:S(2)}, u32[]{:S(2)}) collective-permute-start(bf16[51,2,384]{2,1,0:T(2,128)(2,1)S(1)} %pad_maximum_fusion.refs_0_), channel_id=1, source_target_pairs={{0,2},{1,3},{2,0},{3,1},{4,6},{5,7},{6,4},{7,5},{8,10},{9,11},{10,... | collective-permute-start | bytes 235016 | tf_op jit(solution)/shard_map/ppermute | solution.py:191
  4.8 0.1 collective-permute-start.5
  4.8 3.8 %collective-permute-start = (bf16[2,1024]{1,0:T(2,128)(2,1)}, bf16[2,1024]{1,0:T(2,128)(2,1)S(1)}, u32[]{:S(2)}, u32[]{:S(2)}) collective-permute-start(bf16[2,1024]{1,0:T(2,128)(2,1)} %refs_3_.1), channel_id=1, source_target_pairs={{0,12},{4,8},{8,4},{12,0},{1,13},{5,9},{9,5},{13,1},{2,14},{6,10},... | collective-permute-start | bytes 12296 | tf_op jit(solution)/shard_map/ppermute | solution.py:191
  8.7 0.0 collective-permute-start.1
  8.7 0.0 collective-permute-done.3.refs_1_
  8.7 0.6 %collective-permute-start.2 = (bf16[2,1024]{1,0:T(2,128)(2,1)}, bf16[2,1024]{1,0:T(2,128)(2,1)S(1)}, u32[]{:S(2)}, u32[]{:S(2)}) collective-permute-start(bf16[2,1024]{1,0:T(2,128)(2,1)} %refs_3_.1), channel_id=1, source_target_pairs={{0,4},{4,0},{8,12},{12,8},{1,5},{5,1},{9,13},{13,9},{2,6},{6,2},{1... | collective-permute-start | bytes 12296 | tf_op jit(solution)/shard_map/ppermute | solution.py:191
  9.3 0.0 collective-permute-done.4.refs_2_
  9.3 0.0 collective-permute-done.5.refs_3_
  9.3 1.2 %pick_templates.1.refs_4_ = bf16[1312,512]{1,0:T(8,128)(2,1)S(1)} custom-call(bf16[51,2,384]{2,1,0:T(2,128)(2,1)S(1)} %pad_maximum_fusion.refs_0_, bf16[51,2,384]{2,1,0:T(2,128)(2,1)S(1)} %collective-permute-done.3.refs_1_, bf16[51,2,384]{2,1,0:T(2,128)(2,1)S(1)} %collective-permute-done.4.refs_2_, bf16[51,2,384]{2,1,0:T(2,128)(2,1)S(1)} %collective-permute-done.5.refs_3_), custom_call_target="tpu_custom_call" | custom-call | tf_op jit(solution)/shard_map/pick_templates/pallas_call | solution.py:98
  10.5 0.0 collective-permute-done.refs_0_
  10.5 2.9 %collective-permute-done.1.refs_1_ = bf16[2,1024]{1,0:T(2,128)(2,1)S(1)} collective-permute-done((bf16[2,1024]{1,0:T(2,128)(2,1)}, bf16[2,1024]{1,0:T(2,128)(2,1)S(1)}, u32[]{:S(2)}, u32[]{:S(2)}) %collective-permute-start.1) | collective-permute-done | bytes 4128 | tf_op jit(solution)/shard_map/ppermute | solution.py:191
  13.4 0.0 collective-permute-done.2.refs_2_
  13.4 0.0 copy-done
  13.4 3.2 %harmonic_sums.1 = f32[200,256]{1,0:T(8,128)} custom-call(bf16[2,1024]{1,0:T(2,128)(2,1)S(1)} %collective-permute-done.refs_0_, bf16[2,1024]{1,0:T(2,128)(2,1)S(1)} %collective-permute-done.1.refs_1_, bf16[2,1024]{1,0:T(2,128)(2,1)S(1)} %collective-permute-done.2.refs_2_, bf16[2,1024]{1,0:T(2,128)(2,1)S(1)} %copy-done, ...), custom_call_target="tpu_custom_call" | custom-call | tf_op jit(solution)/shard_map/harmonic_sums/pallas_call | solution.py:173
  (2 shorter events, 0.0 us)
Async XLA Ops:
  0.0 13.4 %copy-start = (bf16[2,1024]{1,0:T(2,128)(2,1)S(1)}, bf16[2,1024]{1,0:T(2,128)(2,1)}, u32[]{:S(2)}) copy-start(bf16[2,1024]{1,0:T(2,128)(2,1)} %refs_3_.1) | copy-start | bytes 12292
  1.7 7.0 %collective-permute-start.3 = (bf16[51,2,384]{2,1,0:T(2,128)(2,1)S(1)}, bf16[51,2,384]{2,1,0:T(2,128)(2,1)S(1)}, u32[]{:S(2)}, u32[]{:S(2)}) collective-permute-start(bf16[51,2,384]{2,1,0:T(2,128)(2,1)S(1)} %pad_maximum_fusion.refs_0_), channel_id=1, source_target_pairs={{0,1},{1,0},{2,3},{3,2},{4,5},{5,4},{6,7},{7,6},{8,9},{9,8},{10,11... | collective-permute-start | bytes 235016 | tf_op jit(solution)/shard_map/ppermute | solution.py:191
  2.2 7.0 %collective-permute-start.4 = (bf16[51,2,384]{2,1,0:T(2,128)(2,1)S(1)}, bf16[51,2,384]{2,1,0:T(2,128)(2,1)S(1)}, u32[]{:S(2)}, u32[]{:S(2)}) collective-permute-start(bf16[51,2,384]{2,1,0:T(2,128)(2,1)S(1)} %pad_maximum_fusion.refs_0_), channel_id=1, source_target_pairs={{0,2},{1,3},{2,0},{3,1},{4,6},{5,7},{6,4},{7,5},{8,10},{9,11},{10,... | collective-permute-start | bytes 235016 | tf_op jit(solution)/shard_map/ppermute | solution.py:191
  4.8 4.5 %collective-permute-start.5 = (bf16[51,2,384]{2,1,0:T(2,128)(2,1)S(1)}, bf16[51,2,384]{2,1,0:T(2,128)(2,1)S(1)}, u32[]{:S(2)}, u32[]{:S(2)}) collective-permute-start(bf16[51,2,384]{2,1,0:T(2,128)(2,1)S(1)} %pad_maximum_fusion.refs_0_), channel_id=1, source_target_pairs={{0,3},{1,2},{2,1},{3,0},{4,7},{5,6},{6,5},{7,4},{8,11},{9,10},{10,... | collective-permute-start | bytes 235016 | tf_op jit(solution)/shard_map/ppermute | solution.py:191
  4.8 5.7 %collective-permute-start = (bf16[2,1024]{1,0:T(2,128)(2,1)}, bf16[2,1024]{1,0:T(2,128)(2,1)S(1)}, u32[]{:S(2)}, u32[]{:S(2)}) collective-permute-start(bf16[2,1024]{1,0:T(2,128)(2,1)} %refs_3_.1), channel_id=1, source_target_pairs={{0,12},{4,8},{8,4},{12,0},{1,13},{5,9},{9,5},{13,1},{2,14},{6,10},... | collective-permute-start | bytes 12296 | tf_op jit(solution)/shard_map/ppermute | solution.py:191
  8.7 4.7 %collective-permute-start.1 = (bf16[2,1024]{1,0:T(2,128)(2,1)}, bf16[2,1024]{1,0:T(2,128)(2,1)S(1)}, u32[]{:S(2)}, u32[]{:S(2)}) collective-permute-start(bf16[2,1024]{1,0:T(2,128)(2,1)} %refs_3_.1), channel_id=1, source_target_pairs={{0,8},{4,12},{8,0},{12,4},{1,9},{5,13},{9,1},{13,5},{2,10},{6,14},... | collective-permute-start | bytes 12296 | tf_op jit(solution)/shard_map/ppermute | solution.py:191
  8.7 4.7 %collective-permute-start.2 = (bf16[2,1024]{1,0:T(2,128)(2,1)}, bf16[2,1024]{1,0:T(2,128)(2,1)S(1)}, u32[]{:S(2)}, u32[]{:S(2)}) collective-permute-start(bf16[2,1024]{1,0:T(2,128)(2,1)} %refs_3_.1), channel_id=1, source_target_pairs={{0,4},{4,0},{8,12},{12,8},{1,5},{5,1},{9,13},{13,9},{2,6},{6,2},{1... | collective-permute-start | bytes 12296 | tf_op jit(solution)/shard_map/ppermute | solution.py:191

commit v4 on v3

--- a/solution.py
+++ b/solution.py
@@ -50,9 +50,7 @@
     return round_up(max(0, -min(low for low, _ in reach)), 8), round_up(max(0, max(high for _, high in reach) + 1 - rows), 8)
 
 
-def pick_kernel(*refs, masks, shard_rows, rows):
-    held = refs[: len(masks)]
-    picked, taps = refs[len(masks) :]
+def place_templates(held, taps, masks, shard_rows, rows):
     acc_index = lax.axis_index("acc")
     tap_tiles = held[0].shape[2] // LANES
     tiles = tap_tiles + 1
@@ -81,45 +79,20 @@
                 taps[part * tiles + tile, pl.ds(first_row, shard_rows), :] = jnp.where(stays, turned, before)
                 before = turned
 
-    centre = rows // 2
-    at = 0
-    for harmonic, (start, count) in enumerate(row_blocks(rows), 1):
-        first_row = before_rows + centre + harmonic * (start - centre)
-        for part in range(2):
-            for tile in range(tiles):
-                chosen = taps[part * tiles + tile, pl.ds(first_row, count, stride=harmonic), :]
-                picked[at : at + count, tile * LANES : (tile + 1) * LANES] = chosen.astype(jnp.bfloat16)
-            at += count
-
-
-def pick_templates(held, masks, rows):
-    shard_rows = held[0].shape[0] - 1
-    picked_rows = 2 * sum(count for _, count in row_blocks(rows))
-    return pl.pallas_call(
-        functools.partial(pick_kernel, masks=masks, shard_rows=shard_rows, rows=rows),
-        out_shape=jax.ShapeDtypeStruct((picked_rows, WIDTH), jnp.bfloat16),
-        in_specs=[VMEM] * len(masks),
-        out_specs=VMEM,
-        scratch_shapes=[pltpu.VMEM((2 * WIDTH // LANES, rows + sum(pick_margins(rows)), LANES), jnp.float32)],
-        compiler_params=pltpu.CompilerParams(vmem_limit_bytes=16 << 20),
-        name="pick_templates",
-    )(*held)
-
-
-def harmonic_kernel(*refs, n_slabs, rows):
-    slabs = refs[:n_slabs]
-    picked, out_ref, line, windows, total = refs[n_slabs:]
-    sub_bins = out_ref.shape[1]
+
+def windows_kernel(*refs):
+    slabs = refs[:-2]
+    windows, line = refs[-2:]
+    sub_bins = windows.shape[2]
     blocks_f = sub_bins // LANES
     window_tiles = WIDTH // LANES
     slab_tiles = slabs[0].shape[1] // LANES
-    filled = n_slabs * slab_tiles
+    filled = len(slabs) * slab_tiles
     freq_index = lax.axis_index("freq")
     acc_index = lax.axis_index("acc")
-    blocks = row_blocks(rows)
 
     line[:, filled:, :] = jnp.zeros((2, line.shape[1] - filled, LANES), jnp.float32)
-    for mask, slab in zip(range(n_slabs - 1, -1, -1), slabs):
+    for mask, slab in zip(range(len(slabs) - 1, -1, -1), slabs):
         values = slab[...].astype(jnp.float32)
         place = (freq_index ^ mask) * slab_tiles
         for tile in range(slab_tiles):
@@ -128,8 +101,6 @@
 
     lane = lax.broadcasted_iota(jnp.int32, (16, LANES), 1)
     sublane = lax.broadcasted_iota(jnp.int32, (16, LANES), 0)
-    total[...] = jnp.zeros_like(total)
-    at = 0
     for harmonic in range(1, H + 1):
         place = lane + harmonic * sublane
         index = place & (LANES - 1)
@@ -141,23 +112,64 @@
             for tile in range(n_tiles + 1):
                 values = jnp.broadcast_to(line[part, pl.ds(first + tile, 1), :], (16, LANES))
                 turned.append(lane_gather(values, index))
-            base = [jnp.where(stays, turned[t], turned[t + 1]).astype(jnp.bfloat16) for t in range(n_tiles)]
-            moved = {0: base}
+            base = [jnp.where(stays, turned[t], turned[t + 1]) for t in range(n_tiles)]
+            moved = {0: [values.astype(jnp.bfloat16) for values in base]}
             for group in range(LANES // 16):
                 tile_by, lane_by = divmod(16 * harmonic * group, LANES)
                 if lane_by not in moved:
                     rolled = [pltpu.roll(values, LANES - lane_by, 1) for values in base]
                     keep = lane < LANES - lane_by
-                    moved[lane_by] = [jnp.where(keep, rolled[t], rolled[min(t + 1, n_tiles - 1)]) for t in range(n_tiles)]
+                    moved[lane_by] = [
+                        jnp.where(keep, rolled[t], rolled[min(t + 1, n_tiles - 1)]).astype(jnp.bfloat16)
+                        for t in range(n_tiles)
+                    ]
                 for block in range(blocks_f):
                     for tile in range(window_tiles):
                         row = block * LANES + 16 * group
                         windows[harmonic - 1, part, row : row + 16, tile * LANES : (tile + 1) * LANES] = moved[lane_by][
                             tile_by + harmonic * block + tile
                         ]
-        start, count = blocks[harmonic - 1]
-        chosen = picked[at : at + 2 * count, :]
-        at += 2 * count
+
+
+def spectrum_windows(slabs, sub_bins):
+    filled = len(slabs) * slabs[0].shape[1] // LANES
+    beyond = WIDTH // LANES + H * (sub_bins // LANES) + 1
+    return pl.pallas_call(
+        windows_kernel,
+        out_shape=jax.ShapeDtypeStruct((H, 2, sub_bins, WIDTH), jnp.bfloat16),
+        in_specs=[VMEM] * len(slabs),
+        out_specs=VMEM,
+        scratch_shapes=[pltpu.VMEM((2, filled + beyond, LANES), jnp.float32)],
+        compiler_params=pltpu.CompilerParams(vmem_limit_bytes=16 << 20),
+        cost_estimate=pl.CostEstimate(flops=10**12, bytes_accessed=4000 << 20, transcendentals=0),
+        name="spectrum_windows",
+    )(*slabs)
+
+
+def sums_kernel(*refs, masks, shard_rows, rows):
+    windows = refs[0]
+    held = refs[1 : len(masks) + 1]
+    out_ref, taps, total = refs[len(masks) + 1 :]
+    place_templates(held, taps, masks, shard_rows, rows)
+    before_rows, _ = pick_margins(rows)
+    tiles = WIDTH // LANES
+    centre = rows // 2
+    total[...] = jnp.zeros_like(total)
+    for harmonic, (start, count) in enumerate(row_blocks(rows), 1):
+        first_row = before_rows + centre + harmonic * (start - centre)
+        chosen = jnp.concatenate(
+            [
+                jnp.concatenate(
+                    [
+                        taps[part * tiles + tile, pl.ds(first_row, count, stride=harmonic), :].astype(jnp.bfloat16)
+                        for tile in range(tiles)
+                    ],
+                    axis=1,
+                )
+                for part in range(2)
+            ],
+            axis=0,
+        )
         with_real = lax.dot_general(chosen, windows[harmonic - 1, 0], NT, preferred_element_type=jnp.float32)
         with_imag = lax.dot_general(chosen, windows[harmonic - 1, 1], NT, preferred_element_type=jnp.float32)
         real = with_real[:count] - with_imag[count:]
@@ -167,22 +179,21 @@
     out_ref[...] = total[:rows, :]
 
 
-def harmonic_sums(slabs, picked, rows, sub_bins):
-    filled = len(slabs) * slabs[0].shape[1] // LANES
-    beyond = WIDTH // LANES + H * (sub_bins // LANES) + 1
+def harmonic_sums(windows, held, masks, rows):
+    shard_rows = held[0].shape[0] - 1
+    sub_bins = windows.shape[2]
     return pl.pallas_call(
-        functools.partial(harmonic_kernel, n_slabs=len(slabs), rows=rows),
+        functools.partial(sums_kernel, masks=masks, shard_rows=shard_rows, rows=rows),
         out_shape=jax.ShapeDtypeStruct((rows, sub_bins), jnp.float32),
-        in_specs=[VMEM] * (len(slabs) + 1),
+        in_specs=[VMEM] * (1 + len(masks)),
         out_specs=VMEM,
         scratch_shapes=[
-            pltpu.VMEM((2, filled + beyond, LANES), jnp.float32),
-            pltpu.VMEM((H, 2, sub_bins, WIDTH), jnp.bfloat16),
+            pltpu.VMEM((2 * WIDTH // LANES, rows + sum(pick_margins(rows)), LANES), jnp.float32),
             pltpu.VMEM((round_up(rows, 16), sub_bins), jnp.float32),
         ],
-        compiler_params=pltpu.CompilerParams(vmem_limit_bytes=32 << 20),
+        compiler_params=pltpu.CompilerParams(vmem_limit_bytes=16 << 20),
         name="harmonic_sums",
-    )(*slabs, picked)
+    )(windows, *held)
 
 
 def exchanged(value, axis):
@@ -194,10 +205,9 @@
 def shards(spectrum, templates, offsets):
     acc_count = lax.axis_size("acc")
     rows = acc_count * templates.shape[1]
-    slabs = exchanged(spectrum, "freq")
+    windows = spectrum_windows(exchanged(spectrum, "freq"), spectrum.shape[1] // acc_count)
     held = exchanged(pack_templates(jnp.transpose(templates, (1, 0, 2)), offsets), "acc")[::-1]
-    picked = pick_templates(held, range(acc_count), rows)
-    return harmonic_sums(slabs, picked, rows, spectrum.shape[1] // acc_count)
+    return harmonic_sums(windows, held, range(acc_count), rows)
 
 
 def solution(mesh):

time: 16.8 us -> 18.5 us (1.10)
  Pallas kernels: 4.45 us -> 5.56 us
  waiting for transfers between devices: 2.89 us -> 2.21 us
  local copies, waits for them, and re-layouts: 0.02 us -> 0.7 us
  other arithmetic: 1.67 us -> 2.28 us
    pallas_call x2, Pallas kernels: 4.45 us -> 5.56 us  [the longest x1 3.66 us: harmonic_sums(): pl.pallas_call(functools.partial(sums_kernel, masks=masks, shard_rows=sha...]
    ppermute x6, waiting for transfers between devices: 2.89 us -> 2.21 us  [exchanged(): lax.ppermute(value, axis, [(i, i ^ mask) for i in range(count)])]
    unnamed x2, local copies, waits for them, and re-layouts: 0.01 us -> 0.69 us
    concatenate x1, other arithmetic: 1 us -> 1.62 us  [pack_templates(): return jnp.concatenate([templates, wide.astype(templates.dtype)], axis=0)]
  transfers between devices with their start and end apart: 6 -> 6, of which waited for: 1 -> 2; matrix products, arithmetic and copies ran while one was open for 0% -> 13% of each run, Pallas kernels for 7% -> 10%
where the time goes in v4:
time: 18.5 us; the launch traced here: 18.2 us
  starting transfers between devices  7.48 us (40%)
  Pallas kernels  5.56 us (30%)
  other arithmetic  2.28 us (12%)
  waiting for transfers between devices  2.21 us (12%)
  local copies, waits for them, and re-layouts  0.7 us (4%)
    ppermute x6, starting transfers between devices, exchanged(): lax.ppermute(value, axis, [(i, i ^ mask) for i in range(count)])  7.48 us
    pallas_call x1, Pallas kernels, harmonic_sums(): pl.pallas_call(functools.partial(sums_kernel, masks=masks, shard_rows=sha...  3.66 us
    ppermute x6, waiting for transfers between devices, exchanged(): lax.ppermute(value, axis, [(i, i ^ mask) for i in range(count)])  2.21 us
    pallas_call x1, Pallas kernels, spectrum_windows(): pl.pallas_call(windows_kernel, out_shape=jax.ShapeDtypeStruct((H, 2, sub_...  1.9 us
    concatenate x1, other arithmetic, pack_templates(): return jnp.concatenate([templates, wide.astype(templates.dtype)], axis=0)  1.62 us
    unnamed x2, local copies, waits for them, and re-layouts  0.69 us
    another operation x1, other arithmetic  0.66 us
  transfers between devices with their start and end apart: 6, of which 2 were waited for; matrix products, arithmetic and copies ran while one was open for 13% of the time, Pallas kernels for 10%

profile of v4, /device:TPU:0, one launch (start us, length us, event | category | flops | bytes accessed | tf_op | source)
XLA Modules:
  0.0 18.2 jit_solution(9497114899327640531)
XLA Ops:
  0.0 4.0 %collective-permute-start.1 = (bf16[2,1024]{1,0:T(2,128)(2,1)}, bf16[2,1024]{1,0:T(2,128)(2,1)S(1)}, u32[]{:S(2)}, u32[]{:S(2)}) collective-permute-start(bf16[2,1024]{1,0:T(2,128)(2,1)} %refs_3_.1), channel_id=1, source_target_pairs={{0,8},{4,12},{8,0},{12,4},{1,9},{5,13},{9,1},{13,5},{2,10},{6,14},... | collective-permute-start | bytes 12296 | tf_op jit(solution)/shard_map/ppermute | solution.py:202
  4.0 1.3 %collective-permute-start = (bf16[2,1024]{1,0:T(2,128)(2,1)}, bf16[2,1024]{1,0:T(2,128)(2,1)S(1)}, u32[]{:S(2)}, u32[]{:S(2)}) collective-permute-start(bf16[2,1024]{1,0:T(2,128)(2,1)} %refs_3_.1), channel_id=1, source_target_pairs={{0,12},{4,8},{8,4},{12,0},{1,13},{5,9},{9,5},{13,1},{2,14},{6,10},... | collective-permute-start | bytes 12296 | tf_op jit(solution)/shard_map/ppermute | solution.py:202
  5.4 0.2 %collective-permute-start.2 = (bf16[2,1024]{1,0:T(2,128)(2,1)}, bf16[2,1024]{1,0:T(2,128)(2,1)S(1)}, u32[]{:S(2)}, u32[]{:S(2)}) collective-permute-start(bf16[2,1024]{1,0:T(2,128)(2,1)} %refs_3_.1), channel_id=1, source_target_pairs={{0,4},{4,0},{8,12},{12,8},{1,5},{5,1},{9,13},{13,9},{2,6},{6,2},{1... | collective-permute-start | bytes 12296 | tf_op jit(solution)/shard_map/ppermute | solution.py:202
  5.6 0.7 %convert.4 = bf16[50]{0:T(256)(128)(2,1)S(1)} convert(s32[50]{0:T(128)} %param.5) | non-fusion elementwise | flops 50 | bytes 300 | tf_op jit(solution)/shard_map/convert
  6.3 1.6 %pad_maximum_fusion.refs_1_ = bf16[51,2,384]{2,1,0:T(2,128)(2,1)} fusion(bf16[1,2,384]{2,1,0:T(2,128)(2,1)S(1)} %broadcast_in_dim.3, bf16[50,2,384]{2,1,0:T(2,128)(2,1)} %bitcast.1), kind=kLoop, calls=%fused_computation | loop fusion | flops 39168 | bytes 156672 | tf_op jit(solution)/shard_map/concatenate | solution.py:41
  7.9 0.4 %collective-permute-start.5 = (bf16[51,2,384]{2,1,0:T(2,128)(2,1)}, bf16[51,2,384]{2,1,0:T(2,128)(2,1)}, u32[]{:S(2)}, u32[]{:S(2)}) collective-permute-start(bf16[51,2,384]{2,1,0:T(2,128)(2,1)} %pad_maximum_fusion.refs_1_), channel_id=1, source_target_pairs={{0,3},{1,2},{2,1},{3,0},{4,7},{5,6},{6,5},{7,4},{8,11},{9,10},{10,... | collective-permute-start | bytes 235016 | tf_op jit(solution)/shard_map/ppermute | solution.py:202
  8.3 1.2 %collective-permute-start.4 = (bf16[51,2,384]{2,1,0:T(2,128)(2,1)}, bf16[51,2,384]{2,1,0:T(2,128)(2,1)}, u32[]{:S(2)}, u32[]{:S(2)}) collective-permute-start(bf16[51,2,384]{2,1,0:T(2,128)(2,1)} %pad_maximum_fusion.refs_1_), channel_id=1, source_target_pairs={{0,2},{1,3},{2,0},{3,1},{4,6},{5,7},{6,4},{7,5},{8,10},{9,11},{10,... | collective-permute-start | bytes 235016 | tf_op jit(solution)/shard_map/ppermute | solution.py:202
  9.4 0.0 collective-permute-done.1.refs_1_
  9.4 0.3 %collective-permute-start.3 = (bf16[51,2,384]{2,1,0:T(2,128)(2,1)}, bf16[51,2,384]{2,1,0:T(2,128)(2,1)}, u32[]{:S(2)}, u32[]{:S(2)}) collective-permute-start(bf16[51,2,384]{2,1,0:T(2,128)(2,1)} %pad_maximum_fusion.refs_1_), channel_id=1, source_target_pairs={{0,1},{1,0},{2,3},{3,2},{4,5},{5,4},{6,7},{7,6},{8,9},{9,8},{10,11... | collective-permute-start | bytes 235016 | tf_op jit(solution)/shard_map/ppermute | solution.py:202
  9.8 0.0 collective-permute-done.refs_0_
  9.8 0.0 collective-permute-done.2.refs_2_
  9.8 0.0 copy-start
  9.8 0.7 %copy-done = bf16[2,1024]{1,0:T(2,128)(2,1)S(1)} copy-done((bf16[2,1024]{1,0:T(2,128)(2,1)S(1)}, bf16[2,1024]{1,0:T(2,128)(2,1)}, u32[]{:S(2)}) %copy-start) | copy-done | bytes 4120
  10.5 1.9 %spectrum_windows.1.refs_0_ = bf16[8,2,256,512]{3,2,1,0:T(8,128)(2,1)S(1)} custom-call(bf16[2,1024]{1,0:T(2,128)(2,1)S(1)} %collective-permute-done.refs_0_, bf16[2,1024]{1,0:T(2,128)(2,1)S(1)} %collective-permute-done.1.refs_1_, bf16[2,1024]{1,0:T(2,128)(2,1)S(1)} %collective-permute-done.2.refs_2_, bf16[2,1024]{1,0:T(2,128)(2,1)S(1)} %copy-done), custom_call_target="tpu_custom_call" | custom-call | flops 999999995904 | bytes 4194304000 | tf_op jit(solution)/shard_map/spectrum_windows/pallas_call | solution.py:137
  12.4 0.5 %collective-permute-done.5.refs_4_ = bf16[51,2,384]{2,1,0:T(2,128)(2,1)} collective-permute-done((bf16[51,2,384]{2,1,0:T(2,128)(2,1)}, bf16[51,2,384]{2,1,0:T(2,128)(2,1)}, u32[]{:S(2)}, u32[]{:S(2)}) %collective-permute-start.5) | collective-permute-done | bytes 78368 | tf_op jit(solution)/shard_map/ppermute | solution.py:202
  12.9 1.7 %collective-permute-done.4.refs_3_ = bf16[51,2,384]{2,1,0:T(2,128)(2,1)} collective-permute-done((bf16[51,2,384]{2,1,0:T(2,128)(2,1)}, bf16[51,2,384]{2,1,0:T(2,128)(2,1)}, u32[]{:S(2)}, u32[]{:S(2)}) %collective-permute-start.4) | collective-permute-done | bytes 78368 | tf_op jit(solution)/shard_map/ppermute | solution.py:202
  14.6 0.0 collective-permute-done.3.refs_2_
  14.6 3.7 %harmonic_sums.1 = f32[200,256]{1,0:T(8,128)} custom-call(bf16[8,2,256,512]{3,2,1,0:T(8,128)(2,1)S(1)} %spectrum_windows.1.refs_0_, bf16[51,2,384]{2,1,0:T(2,128)(2,1)} %pad_maximum_fusion.refs_1_, bf16[51,2,384]{2,1,0:T(2,128)(2,1)} %collective-permute-done.3.refs_2_, bf16[51,2,384]{2,1,0:T(2,128)(2,1)} %collective-permute-done.4.refs_3_, ...), custom_call_target="tpu_custom_call" | custom-call | tf_op jit(solution)/shard_map/harmonic_sums/pallas_call | solution.py:185
  (2 shorter events, 0.0 us)
Async XLA Ops:
  0.0 9.4 %collective-permute-start.1 = (bf16[2,1024]{1,0:T(2,128)(2,1)}, bf16[2,1024]{1,0:T(2,128)(2,1)S(1)}, u32[]{:S(2)}, u32[]{:S(2)}) collective-permute-start(bf16[2,1024]{1,0:T(2,128)(2,1)} %refs_3_.1), channel_id=1, source_target_pairs={{0,8},{4,12},{8,0},{12,4},{1,9},{5,13},{9,1},{13,5},{2,10},{6,14},... | collective-permute-start | bytes 12296 | tf_op jit(solution)/shard_map/ppermute | solution.py:202
  4.0 5.7 %collective-permute-start = (bf16[2,1024]{1,0:T(2,128)(2,1)}, bf16[2,1024]{1,0:T(2,128)(2,1)S(1)}, u32[]{:S(2)}, u32[]{:S(2)}) collective-permute-start(bf16[2,1024]{1,0:T(2,128)(2,1)} %refs_3_.1), channel_id=1, source_target_pairs={{0,12},{4,8},{8,4},{12,0},{1,13},{5,9},{9,5},{13,1},{2,14},{6,10},... | collective-permute-start | bytes 12296 | tf_op jit(solution)/shard_map/ppermute | solution.py:202
  5.4 4.4 %collective-permute-start.2 = (bf16[2,1024]{1,0:T(2,128)(2,1)}, bf16[2,1024]{1,0:T(2,128)(2,1)S(1)}, u32[]{:S(2)}, u32[]{:S(2)}) collective-permute-start(bf16[2,1024]{1,0:T(2,128)(2,1)} %refs_3_.1), channel_id=1, source_target_pairs={{0,4},{4,0},{8,12},{12,8},{1,5},{5,1},{9,13},{13,9},{2,6},{6,2},{1... | collective-permute-start | bytes 12296 | tf_op jit(solution)/shard_map/ppermute | solution.py:202
  7.9 4.9 %collective-permute-start.5 = (bf16[51,2,384]{2,1,0:T(2,128)(2,1)}, bf16[51,2,384]{2,1,0:T(2,128)(2,1)}, u32[]{:S(2)}, u32[]{:S(2)}) collective-permute-start(bf16[51,2,384]{2,1,0:T(2,128)(2,1)} %pad_maximum_fusion.refs_1_), channel_id=1, source_target_pairs={{0,3},{1,2},{2,1},{3,0},{4,7},{5,6},{6,5},{7,4},{8,11},{9,10},{10,... | collective-permute-start | bytes 235016 | tf_op jit(solution)/shard_map/ppermute | solution.py:202
  8.3 6.3 %collective-permute-start.4 = (bf16[51,2,384]{2,1,0:T(2,128)(2,1)}, bf16[51,2,384]{2,1,0:T(2,128)(2,1)}, u32[]{:S(2)}, u32[]{:S(2)}) collective-permute-start(bf16[51,2,384]{2,1,0:T(2,128)(2,1)} %pad_maximum_fusion.refs_1_), channel_id=1, source_target_pairs={{0,2},{1,3},{2,0},{3,1},{4,6},{5,7},{6,4},{7,5},{8,10},{9,11},{10,... | collective-permute-start | bytes 235016 | tf_op jit(solution)/shard_map/ppermute | solution.py:202
  9.4 5.1 %collective-permute-start.3 = (bf16[51,2,384]{2,1,0:T(2,128)(2,1)}, bf16[51,2,384]{2,1,0:T(2,128)(2,1)}, u32[]{:S(2)}, u32[]{:S(2)}) collective-permute-start(bf16[51,2,384]{2,1,0:T(2,128)(2,1)} %pad_maximum_fusion.refs_1_), channel_id=1, source_target_pairs={{0,1},{1,0},{2,3},{3,2},{4,5},{5,4},{6,7},{7,6},{8,9},{9,8},{10,11... | collective-permute-start | bytes 235016 | tf_op jit(solution)/shard_map/ppermute | solution.py:202
  9.8 0.7 %copy-start = (bf16[2,1024]{1,0:T(2,128)(2,1)S(1)}, bf16[2,1024]{1,0:T(2,128)(2,1)}, u32[]{:S(2)}) copy-start(bf16[2,1024]{1,0:T(2,128)(2,1)} %refs_3_.1) | copy-start | bytes 12292

commit v5 on v3

--- a/solution.py
+++ b/solution.py
@@ -119,9 +119,10 @@
     blocks = row_blocks(rows)
 
     line[:, filled:, :] = jnp.zeros((2, line.shape[1] - filled, LANES), jnp.float32)
-    for mask, slab in zip(range(n_slabs - 1, -1, -1), slabs):
+    for (even, odd), slab in zip(slab_slots(n_slabs), slabs):
         values = slab[...].astype(jnp.float32)
-        place = (freq_index ^ mask) * slab_tiles
+        ahead = even + (odd - even) * (acc_index & 1)
+        place = lax.rem(freq_index + ahead, n_slabs) * slab_tiles
         for tile in range(slab_tiles):
             for part in range(2):
                 line[part, pl.ds(place + tile, 1), :] = values[part : part + 1, tile * LANES : (tile + 1) * LANES]
@@ -129,8 +130,11 @@
     lane = lax.broadcasted_iota(jnp.int32, (16, LANES), 1)
     sublane = lax.broadcasted_iota(jnp.int32, (16, LANES), 0)
     total[...] = jnp.zeros_like(total)
-    at = 0
-    for harmonic in range(1, H + 1):
+    at = [0]
+    for _, count in blocks:
+        at.append(at[-1] + 2 * count)
+
+    def build(harmonic):
         place = lane + harmonic * sublane
         index = place & (LANES - 1)
         stays = place < LANES
@@ -141,29 +145,37 @@
             for tile in range(n_tiles + 1):
                 values = jnp.broadcast_to(line[part, pl.ds(first + tile, 1), :], (16, LANES))
                 turned.append(lane_gather(values, index))
-            base = [jnp.where(stays, turned[t], turned[t + 1]).astype(jnp.bfloat16) for t in range(n_tiles)]
-            moved = {0: base}
+            base = [jnp.where(stays, turned[t], turned[t + 1]) for t in range(n_tiles)]
+            moved = {0: [values.astype(jnp.bfloat16) for values in base]}
             for group in range(LANES // 16):
                 tile_by, lane_by = divmod(16 * harmonic * group, LANES)
                 if lane_by not in moved:
                     rolled = [pltpu.roll(values, LANES - lane_by, 1) for values in base]
                     keep = lane < LANES - lane_by
-                    moved[lane_by] = [jnp.where(keep, rolled[t], rolled[min(t + 1, n_tiles - 1)]) for t in range(n_tiles)]
+                    moved[lane_by] = [
+                        jnp.where(keep, rolled[t], rolled[min(t + 1, n_tiles - 1)]).astype(jnp.bfloat16)
+                        for t in range(n_tiles)
+                    ]
                 for block in range(blocks_f):
                     for tile in range(window_tiles):
                         row = block * LANES + 16 * group
                         windows[harmonic - 1, part, row : row + 16, tile * LANES : (tile + 1) * LANES] = moved[lane_by][
                             tile_by + harmonic * block + tile
                         ]
+
+    def multiply(harmonic):
         start, count = blocks[harmonic - 1]
-        chosen = picked[at : at + 2 * count, :]
-        at += 2 * count
+        chosen = picked[at[harmonic - 1] : at[harmonic], :]
         with_real = lax.dot_general(chosen, windows[harmonic - 1, 0], NT, preferred_element_type=jnp.float32)
         with_imag = lax.dot_general(chosen, windows[harmonic - 1, 1], NT, preferred_element_type=jnp.float32)
         real = with_real[:count] - with_imag[count:]
         imag = with_imag[:count] + with_real[count:]
         power = (real * real + imag * imag).astype(jnp.bfloat16)
         total[start : start + count, :] += power.astype(jnp.float32)
+
+    for harmonic in range(1, H + 1):
+        build(harmonic)
+        multiply(harmonic)
     out_ref[...] = total[:rows, :]
 
 
@@ -185,17 +197,42 @@
     )(*slabs, picked)
 
 
-def exchanged(value, axis):
-    count = lax.axis_size(axis)
-    masks = range(count - 1, 0, -1)
-    return [lax.ppermute(value, axis, [(i, i ^ mask) for i in range(count)]) for mask in masks] + [value]
+def slab_steps(freq_count):
+    ahead = list(range(freq_count - 1, 0, -1))
+    return [(ahead[i], ahead[min(i + 1, len(ahead) - 1)]) for i in range(0, len(ahead), 2)]
+
+
+def slab_slots(freq_count):
+    steps = slab_steps(freq_count)
+    return steps + [(odd, even) for even, odd in steps if even != odd] + [(0, 0)]
+
+
+def swapped(value, mask):
+    return lax.ppermute(value, "acc", [(i, i ^ mask) for i in range(lax.axis_size("acc"))])
+
+
+def gathered_slabs(spectrum):
+    freq_count, acc_count = lax.axis_size("freq"), lax.axis_size("acc")
+    fetched = []
+    for step in slab_steps(freq_count):
+        pairs = [
+            ((i + step[a % 2]) % freq_count * acc_count + a, i * acc_count + a)
+            for i in range(freq_count)
+            for a in range(acc_count)
+        ]
+        fetched.append(lax.ppermute(spectrum, ("freq", "acc"), pairs))
+    return fetched + [swapped(slab, 1) for slab, step in zip(fetched, slab_steps(freq_count)) if step[0] != step[1]] + [spectrum]
+
+
+def gathered_templates(packed):
+    return [packed] + [swapped(packed, mask) for mask in range(1, lax.axis_size("acc"))]
 
 
 def shards(spectrum, templates, offsets):
     acc_count = lax.axis_size("acc")
     rows = acc_count * templates.shape[1]
-    slabs = exchanged(spectrum, "freq")
-    held = exchanged(pack_templates(jnp.transpose(templates, (1, 0, 2)), offsets), "acc")[::-1]
+    slabs = gathered_slabs(spectrum)
+    held = gathered_templates(pack_templates(jnp.transpose(templates, (1, 0, 2)), offsets))
     picked = pick_templates(held, range(acc_count), rows)
     return harmonic_sums(slabs, picked, rows, spectrum.shape[1] // acc_count)
 

time: 16.8 us -> 15 us (0.89)
  waiting for transfers between devices: 2.89 us -> 1.85 us
  starting transfers between devices: 7.56 us -> 6.99 us
  Pallas kernels: 4.45 us -> 4.18 us
    ppermute x6, waiting for transfers between devices: 2.89 us -> 1.85 us  [the longest x2 1.84 us: gathered_slabs(): fetched.append(lax.ppermute(spectrum, ('freq', 'acc'), pairs))]
    ppermute x6, starting transfers between devices: 7.56 us -> 6.99 us  [the longest x2 3.84 us: gathered_slabs(): fetched.append(lax.ppermute(spectrum, ('freq', 'acc'), pairs))]
    pallas_call x1, Pallas kernels: 3.2 us -> 2.94 us  [harmonic_sums(): pl.pallas_call(functools.partial(harmonic_kernel, n_slabs=len(slabs), row...]
  transfers between devices with their start and end apart: 6 -> 6, of which waited for: 1 -> 1; matrix products, arithmetic and copies ran while one was open for 0% -> 0% of each run, Pallas kernels for 7% -> 8%
where the time goes in v5:
time: 15 us; the launch traced here: 14.8 us
  starting transfers between devices  6.99 us (47%)
  Pallas kernels  4.18 us (28%)
  waiting for transfers between devices  1.85 us (12%)
  other arithmetic  1.67 us (11%)
    ppermute x2, starting transfers between devices, gathered_slabs(): fetched.append(lax.ppermute(spectrum, ('freq', 'acc'), pairs))  3.84 us
    ppermute x4, starting transfers between devices, swapped(): lax.ppermute(value, 'acc', [(i, i ^ mask) for i in range(lax.axis_size('a...  3.15 us
    pallas_call x1, Pallas kernels, harmonic_sums(): pl.pallas_call(functools.partial(harmonic_kernel, n_slabs=len(slabs), row...  2.94 us
    ppermute x2, waiting for transfers between devices, gathered_slabs(): fetched.append(lax.ppermute(spectrum, ('freq', 'acc'), pairs))  1.84 us
    pallas_call x1, Pallas kernels, pick_templates(): pl.pallas_call(functools.partial(pick_kernel, masks=masks, shard_rows=sha...  1.24 us
    concatenate x1, other arithmetic, pack_templates(): return jnp.concatenate([templates, wide.astype(templates.dtype)], axis=0)  1 us
    another operation x1, other arithmetic  0.67 us
  transfers between devices with their start and end apart: 6, of which 1 were waited for; matrix products, arithmetic and copies ran while one was open for 0% of the time, Pallas kernels for 8%

profile of v5, /device:TPU:0, one launch (start us, length us, event | category | flops | bytes accessed | tf_op | source)
XLA Modules:
  0.0 14.8 jit_solution(5856940843574348678)
XLA Ops:
  0.0 0.0 copy-start
  0.0 0.7 %convert.4 = bf16[50]{0:T(256)(128)(2,1)S(1)} convert(s32[50]{0:T(128)} %param.5) | non-fusion elementwise | flops 50 | bytes 300 | tf_op jit(solution)/shard_map/convert
  0.7 1.0 %pad_maximum_fusion.refs_0_ = bf16[51,2,384]{2,1,0:T(2,128)(2,1)S(1)} fusion(bf16[1,2,384]{2,1,0:T(2,128)(2,1)S(1)} %broadcast_in_dim.3, bf16[50,2,384]{2,1,0:T(2,128)(2,1)} %bitcast.1), kind=kLoop, calls=%fused_computation | loop fusion | flops 39168 | bytes 156672 | tf_op jit(solution)/shard_map/concatenate | solution.py:41
  1.7 0.5 %collective-permute-start.3 = (bf16[51,2,384]{2,1,0:T(2,128)(2,1)S(1)}, bf16[51,2,384]{2,1,0:T(2,128)(2,1)S(1)}, u32[]{:S(2)}, u32[]{:S(2)}) collective-permute-start(bf16[51,2,384]{2,1,0:T(2,128)(2,1)S(1)} %pad_maximum_fusion.refs_0_), channel_id=1, source_target_pairs={{0,1},{1,0},{2,3},{3,2},{4,5},{5,4},{6,7},{7,6},{8,9},{9,8},{10,11... | collective-permute-start | bytes 235016 | tf_op jit(solution)/shard_map/ppermute | solution.py:211
  2.2 2.6 %collective-permute-start.4 = (bf16[51,2,384]{2,1,0:T(2,128)(2,1)S(1)}, bf16[51,2,384]{2,1,0:T(2,128)(2,1)S(1)}, u32[]{:S(2)}, u32[]{:S(2)}) collective-permute-start(bf16[51,2,384]{2,1,0:T(2,128)(2,1)S(1)} %pad_maximum_fusion.refs_0_), channel_id=1, source_target_pairs={{0,2},{1,3},{2,0},{3,1},{4,6},{5,7},{6,4},{7,5},{8,10},{9,11},{10,... | collective-permute-start | bytes 235016 | tf_op jit(solution)/shard_map/ppermute | solution.py:211
  4.8 0.1 collective-permute-start.5
  4.8 1.8 %collective-permute-start = (bf16[2,1024]{1,0:T(2,128)(2,1)}, bf16[2,1024]{1,0:T(2,128)(2,1)S(1)}, u32[]{:S(2)}, u32[]{:S(2)}) collective-permute-start(bf16[2,1024]{1,0:T(2,128)(2,1)} %refs_3_.1), channel_id=1, source_target_pairs={{12,0},{9,1},{14,2},{11,3},{0,4},{13,5},{2,6},{15,7},{4,8},{1,9},{... | collective-permute-start | bytes 12296 | tf_op jit(solution)/shard_map/ppermute | solution.py:223
  6.7 2.0 %collective-permute-start.1 = (bf16[2,1024]{1,0:T(2,128)(2,1)}, bf16[2,1024]{1,0:T(2,128)(2,1)S(1)}, u32[]{:S(2)}, u32[]{:S(2)}) collective-permute-start(bf16[2,1024]{1,0:T(2,128)(2,1)} %refs_3_.1), channel_id=1, source_target_pairs={{4,0},{5,1},{6,2},{7,3},{8,4},{9,5},{10,6},{11,7},{12,8},{13,9},{1... | collective-permute-start | bytes 12296 | tf_op jit(solution)/shard_map/ppermute | solution.py:223
  8.7 1.8 %collective-permute-done.refs_0_ = bf16[2,1024]{1,0:T(2,128)(2,1)S(1)} collective-permute-done((bf16[2,1024]{1,0:T(2,128)(2,1)}, bf16[2,1024]{1,0:T(2,128)(2,1)S(1)}, u32[]{:S(2)}, u32[]{:S(2)}) %collective-permute-start) | collective-permute-done | bytes 4128 | tf_op jit(solution)/shard_map/ppermute | solution.py:223
  10.5 0.0 collective-permute-start.2
  10.5 0.0 collective-permute-done.3.refs_1_
  10.5 0.0 collective-permute-done.4.refs_2_
  10.5 0.0 collective-permute-done.5.refs_3_
  10.5 1.2 %pick_templates.1.refs_4_ = bf16[1312,512]{1,0:T(8,128)(2,1)S(1)} custom-call(bf16[51,2,384]{2,1,0:T(2,128)(2,1)S(1)} %pad_maximum_fusion.refs_0_, bf16[51,2,384]{2,1,0:T(2,128)(2,1)S(1)} %collective-permute-done.3.refs_1_, bf16[51,2,384]{2,1,0:T(2,128)(2,1)S(1)} %collective-permute-done.4.refs_2_, bf16[51,2,384]{2,1,0:T(2,128)(2,1)S(1)} %collective-permute-done.5.refs_3_), custom_call_target="tpu_custom_call" | custom-call | tf_op jit(solution)/shard_map/pick_templates/pallas_call | solution.py:98
  11.8 0.0 collective-permute-done.1.refs_1_
  11.8 0.0 collective-permute-done.2.refs_2_
  11.8 0.0 copy-done
  11.8 2.9 %harmonic_sums.1 = f32[200,256]{1,0:T(8,128)} custom-call(bf16[2,1024]{1,0:T(2,128)(2,1)S(1)} %collective-permute-done.refs_0_, bf16[2,1024]{1,0:T(2,128)(2,1)S(1)} %collective-permute-done.1.refs_1_, bf16[2,1024]{1,0:T(2,128)(2,1)S(1)} %collective-permute-done.2.refs_2_, bf16[2,1024]{1,0:T(2,128)(2,1)S(1)} %copy-done, ...), custom_call_target="tpu_custom_call" | custom-call | tf_op jit(solution)/shard_map/harmonic_sums/pallas_call | solution.py:185
  (2 shorter events, 0.0 us)
Async XLA Ops:
  0.0 11.8 %copy-start = (bf16[2,1024]{1,0:T(2,128)(2,1)S(1)}, bf16[2,1024]{1,0:T(2,128)(2,1)}, u32[]{:S(2)}) copy-start(bf16[2,1024]{1,0:T(2,128)(2,1)} %refs_3_.1) | copy-start | bytes 12292
  1.7 8.8 %collective-permute-start.3 = (bf16[51,2,384]{2,1,0:T(2,128)(2,1)S(1)}, bf16[51,2,384]{2,1,0:T(2,128)(2,1)S(1)}, u32[]{:S(2)}, u32[]{:S(2)}) collective-permute-start(bf16[51,2,384]{2,1,0:T(2,128)(2,1)S(1)} %pad_maximum_fusion.refs_0_), channel_id=1, source_target_pairs={{0,1},{1,0},{2,3},{3,2},{4,5},{5,4},{6,7},{7,6},{8,9},{9,8},{10,11... | collective-permute-start | bytes 235016 | tf_op jit(solution)/shard_map/ppermute | solution.py:211
  2.2 8.3 %collective-permute-start.4 = (bf16[51,2,384]{2,1,0:T(2,128)(2,1)S(1)}, bf16[51,2,384]{2,1,0:T(2,128)(2,1)S(1)}, u32[]{:S(2)}, u32[]{:S(2)}) collective-permute-start(bf16[51,2,384]{2,1,0:T(2,128)(2,1)S(1)} %pad_maximum_fusion.refs_0_), channel_id=1, source_target_pairs={{0,2},{1,3},{2,0},{3,1},{4,6},{5,7},{6,4},{7,5},{8,10},{9,11},{10,... | collective-permute-start | bytes 235016 | tf_op jit(solution)/shard_map/ppermute | solution.py:211
  4.8 5.8 %collective-permute-start.5 = (bf16[51,2,384]{2,1,0:T(2,128)(2,1)S(1)}, bf16[51,2,384]{2,1,0:T(2,128)(2,1)S(1)}, u32[]{:S(2)}, u32[]{:S(2)}) collective-permute-start(bf16[51,2,384]{2,1,0:T(2,128)(2,1)S(1)} %pad_maximum_fusion.refs_0_), channel_id=1, source_target_pairs={{0,3},{1,2},{2,1},{3,0},{4,7},{5,6},{6,5},{7,4},{8,11},{9,10},{10,... | collective-permute-start | bytes 235016 | tf_op jit(solution)/shard_map/ppermute | solution.py:211
  4.8 5.7 %collective-permute-start = (bf16[2,1024]{1,0:T(2,128)(2,1)}, bf16[2,1024]{1,0:T(2,128)(2,1)S(1)}, u32[]{:S(2)}, u32[]{:S(2)}) collective-permute-start(bf16[2,1024]{1,0:T(2,128)(2,1)} %refs_3_.1), channel_id=1, source_target_pairs={{12,0},{9,1},{14,2},{11,3},{0,4},{13,5},{2,6},{15,7},{4,8},{1,9},{... | collective-permute-start | bytes 12296 | tf_op jit(solution)/shard_map/ppermute | solution.py:223
  6.7 5.1 %collective-permute-start.1 = (bf16[2,1024]{1,0:T(2,128)(2,1)}, bf16[2,1024]{1,0:T(2,128)(2,1)S(1)}, u32[]{:S(2)}, u32[]{:S(2)}) collective-permute-start(bf16[2,1024]{1,0:T(2,128)(2,1)} %refs_3_.1), channel_id=1, source_target_pairs={{4,0},{5,1},{6,2},{7,3},{8,4},{9,5},{10,6},{11,7},{12,8},{13,9},{1... | collective-permute-start | bytes 12296 | tf_op jit(solution)/shard_map/ppermute | solution.py:223
  10.5 1.3 %collective-permute-start.2 = (bf16[2,1024]{1,0:T(2,128)(2,1)S(1)}, bf16[2,1024]{1,0:T(2,128)(2,1)S(1)}, u32[]{:S(2)}, u32[]{:S(2)}) collective-permute-start(bf16[2,1024]{1,0:T(2,128)(2,1)S(1)} %collective-permute-done.refs_0_), channel_id=1, source_target_pairs={{0,1},{1,0},{2,3},{3,2},{4,5},{5,4},{6,7},{7,6},{8,9},{9,8},{10,11... | collective-permute-start | bytes 12296 | tf_op jit(solution)/shard_map/ppermute | solution.py:211

commit v6 on v5

--- a/solution.py
+++ b/solution.py
@@ -50,36 +50,63 @@
     return round_up(max(0, -min(low for low, _ in reach)), 8), round_up(max(0, max(high for _, high in reach) + 1 - rows), 8)
 
 
+def shift_kernel(packed_ref, out_ref):
+    shard_rows = out_ref.shape[1]
+    shift_rows(packed_ref, out_ref, pl.ds(0, shard_rows), shard_rows)
+
+
+def shift_rows(packed_ref, out_ref, place, shard_rows):
+    tap_tiles = packed_ref.shape[2] // LANES
+    tiles = tap_tiles + 1
+    lane = lax.broadcasted_iota(jnp.int32, (shard_rows, LANES), 1)
+    spot = lax.broadcasted_iota(jnp.int32, (shard_rows, shard_rows), 0) == lax.broadcasted_iota(
+        jnp.int32, (shard_rows, shard_rows), 1
+    )
+    packed = packed_ref[shard_rows, 0:1, :shard_rows].astype(jnp.float32)
+    offset = jnp.sum(jnp.where(spot, packed, 0.0), axis=1, keepdims=True)
+    offset = jnp.broadcast_to(offset.astype(jnp.int32), (shard_rows, LANES))
+    index = (lane - offset) & (LANES - 1)
+    stays = lane >= offset
+    for part in range(2):
+        values = packed_ref[:shard_rows, part, :].astype(jnp.float32)
+        before = jnp.zeros((shard_rows, LANES), jnp.float32)
+        for tile in range(tiles):
+            if tile < tap_tiles:
+                turned = lane_gather(values[:, tile * LANES : (tile + 1) * LANES], index)
+            else:
+                turned = jnp.zeros((shard_rows, LANES), jnp.float32)
+            out_ref[part * tiles + tile, place, :] = jnp.where(stays, turned, before)
+            before = turned
+
+
+def shift_own(packed):
+    shard_rows = packed.shape[0] - 1
+    return pl.pallas_call(
+        shift_kernel,
+        out_shape=jax.ShapeDtypeStruct((2 * WIDTH // LANES, shard_rows, LANES), jnp.float32),
+        in_specs=[VMEM],
+        out_specs=VMEM,
+        compiler_params=pltpu.CompilerParams(vmem_limit_bytes=4 << 20),
+        cost_estimate=pl.CostEstimate(flops=2 * 10**9, bytes_accessed=1 << 20, transcendentals=0),
+        name="shift_own",
+    )(packed)
+
+
 def pick_kernel(*refs, masks, shard_rows, rows):
     held = refs[: len(masks)]
     picked, taps = refs[len(masks) :]
     acc_index = lax.axis_index("acc")
-    tap_tiles = held[0].shape[2] // LANES
-    tiles = tap_tiles + 1
+    tiles = WIDTH // LANES
     before_rows, after_rows = pick_margins(rows)
-    lane = lax.broadcasted_iota(jnp.int32, (shard_rows, LANES), 1)
-    spot = lax.broadcasted_iota(jnp.int32, (shard_rows, shard_rows), 0) == lax.broadcasted_iota(
-        jnp.int32, (shard_rows, shard_rows), 1
-    )
     taps[:, :before_rows, :] = jnp.zeros((2 * tiles, before_rows, LANES), jnp.float32)
     taps[:, before_rows + rows :, :] = jnp.zeros((2 * tiles, taps.shape[1] - before_rows - rows, LANES), jnp.float32)
     for slot, mask in enumerate(masks):
-        packed = held[slot][shard_rows, 0:1, :shard_rows].astype(jnp.float32)
-        offset = jnp.sum(jnp.where(spot, packed, 0.0), axis=1, keepdims=True)
-        offset = jnp.broadcast_to(offset.astype(jnp.int32), (shard_rows, LANES))
-        index = (lane - offset) & (LANES - 1)
-        stays = lane >= offset
-        first_row = before_rows + (acc_index ^ mask) * shard_rows
-        for part in range(2):
-            values = held[slot][:shard_rows, part, :].astype(jnp.float32)
-            before = jnp.zeros((shard_rows, LANES), jnp.float32)
-            for tile in range(tiles):
-                if tile < tap_tiles:
-                    turned = lane_gather(values[:, tile * LANES : (tile + 1) * LANES], index)
-                else:
-                    turned = jnp.zeros((shard_rows, LANES), jnp.float32)
-                taps[part * tiles + tile, pl.ds(first_row, shard_rows), :] = jnp.where(stays, turned, before)
-                before = turned
+        place = pl.ds(before_rows + (acc_index ^ mask) * shard_rows, shard_rows)
+        if slot == 0:
+            for tile in range(2 * tiles):
+                taps[tile, place, :] = held[0][tile]
+        else:
+            shift_rows(held[slot], taps, place, shard_rows)
 
     centre = rows // 2
     at = 0
@@ -93,7 +120,7 @@
 
 
 def pick_templates(held, masks, rows):
-    shard_rows = held[0].shape[0] - 1
+    shard_rows = held[0].shape[1]
     picked_rows = 2 * sum(count for _, count in row_blocks(rows))
     return pl.pallas_call(
         functools.partial(pick_kernel, masks=masks, shard_rows=shard_rows, rows=rows),
@@ -219,13 +246,14 @@
             ((i + step[a % 2]) % freq_count * acc_count + a, i * acc_count + a)
             for i in range(freq_count)
             for a in range(acc_count)
+            if i + step[a % 2] < freq_count
         ]
         fetched.append(lax.ppermute(spectrum, ("freq", "acc"), pairs))
     return fetched + [swapped(slab, 1) for slab, step in zip(fetched, slab_steps(freq_count)) if step[0] != step[1]] + [spectrum]
 
 
 def gathered_templates(packed):
-    return [packed] + [swapped(packed, mask) for mask in range(1, lax.axis_size("acc"))]
+    return [shift_own(packed)] + [swapped(packed, mask) for mask in range(1, lax.axis_size("acc"))]
 
 
 def shards(spectrum, templates, offsets):

time: 15 us -> 15 us (level)
  starting transfers between devices: 6.99 us -> 5.71 us
  waiting for transfers between devices: 1.85 us -> 3.11 us
    ppermute x4, waiting for transfers between devices: 0.01 us -> 1.98 us  [swapped(): lax.ppermute(value, 'acc', [(i, i ^ mask) for i in range(lax.axis_size('a...]
    ppermute x2, starting transfers between devices: 3.84 us -> 2.56 us  [gathered_slabs(): fetched.append(lax.ppermute(spectrum, ('freq', 'acc'), pairs))]
    ppermute x2, waiting for transfers between devices: 1.84 us -> 1.13 us  [gathered_slabs(): fetched.append(lax.ppermute(spectrum, ('freq', 'acc'), pairs))]
    pallas_call x0 -> x1, Pallas kernels: none -> 0.26 us  [shift_own(): pl.pallas_call(shift_kernel, out_shape=jax.ShapeDtypeStruct((2 * WIDTH //...]
    pallas_call x1, Pallas kernels: 1.24 us -> 1.02 us  [pick_templates(): pl.pallas_call(functools.partial(pick_kernel, masks=masks, shard_rows=sha...]
  transfers between devices with their start and end apart: 6 -> 6, of which waited for: 1 -> 4; matrix products, arithmetic and copies ran while one was open for 0% -> 11% of each run, Pallas kernels for 8% -> 9%
where the time goes in v6:
time: 15 us; the launch traced here: 14.8 us
  starting transfers between devices  5.71 us (38%)
  Pallas kernels  4.21 us (28%)
  waiting for transfers between devices  3.11 us (21%)
  other arithmetic  1.66 us (11%)
    ppermute x4, starting transfers between devices, swapped(): lax.ppermute(value, 'acc', [(i, i ^ mask) for i in range(lax.axis_size('a...  3.15 us
    pallas_call x1, Pallas kernels, harmonic_sums(): pl.pallas_call(functools.partial(harmonic_kernel, n_slabs=len(slabs), row...  2.93 us
    ppermute x2, starting transfers between devices, gathered_slabs(): fetched.append(lax.ppermute(spectrum, ('freq', 'acc'), pairs))  2.56 us
    ppermute x4, waiting for transfers between devices, swapped(): lax.ppermute(value, 'acc', [(i, i ^ mask) for i in range(lax.axis_size('a...  1.98 us
    ppermute x2, waiting for transfers between devices, gathered_slabs(): fetched.append(lax.ppermute(spectrum, ('freq', 'acc'), pairs))  1.13 us
    pallas_call x1, Pallas kernels, pick_templates(): pl.pallas_call(functools.partial(pick_kernel, masks=masks, shard_rows=sha...  1.02 us
    concatenate x1, other arithmetic, pack_templates(): return jnp.concatenate([templates, wide.astype(templates.dtype)], axis=0)  1 us
    another operation x1, other arithmetic  0.66 us
  transfers between devices with their start and end apart: 6, of which 4 were waited for; matrix products, arithmetic and copies ran while one was open for 11% of the time, Pallas kernels for 9%

profile of v6, /device:TPU:0, one launch (start us, length us, event | category | flops | bytes accessed | tf_op | source)
XLA Modules:
  0.0 14.8 jit_solution(7323522734563025914)
XLA Ops:
  0.0 1.3 %collective-permute-start = (bf16[2,1024]{1,0:T(2,128)(2,1)}, bf16[2,1024]{1,0:T(2,128)(2,1)S(1)}, u32[]{:S(2)}, u32[]{:S(2)}) collective-permute-start(bf16[2,1024]{1,0:T(2,128)(2,1)} %refs_3_.1), channel_id=1, source_target_pairs={{12,0},{9,1},{14,2},{11,3},{13,5},{15,7},{28,16},{25,17},{30,18},{... | collective-permute-start | bytes 12296 | tf_op jit(solution)/shard_map/ppermute | solution.py:251
  1.3 0.7 %convert.4 = bf16[50]{0:T(256)(128)(2,1)S(1)} convert(s32[50]{0:T(128)} %param.5) | non-fusion elementwise | flops 50 | bytes 300 | tf_op jit(solution)/shard_map/convert
  2.0 1.0 %pad_maximum_fusion.packed_ref = bf16[51,2,384]{2,1,0:T(2,128)(2,1)S(1)} fusion(bf16[1,2,384]{2,1,0:T(2,128)(2,1)S(1)} %broadcast_in_dim.3, bf16[50,2,384]{2,1,0:T(2,128)(2,1)} %bitcast.1), kind=kLoop, calls=%fused_computation | loop fusion | flops 39168 | bytes 156672 | tf_op jit(solution)/shard_map/concatenate | solution.py:41
  3.0 0.5 %collective-permute-start.3 = (bf16[51,2,384]{2,1,0:T(2,128)(2,1)S(1)}, bf16[51,2,384]{2,1,0:T(2,128)(2,1)S(1)}, u32[]{:S(2)}, u32[]{:S(2)}) collective-permute-start(bf16[51,2,384]{2,1,0:T(2,128)(2,1)S(1)} %pad_maximum_fusion.packed_ref), channel_id=1, source_target_pairs={{0,1},{1,0},{2,3},{3,2},{4,5},{5,4},{6,7},{7,6},{8,9},{9,8},{10,11... | collective-permute-start | bytes 235016 | tf_op jit(solution)/shard_map/ppermute | solution.py:238
  3.5 2.6 %collective-permute-start.4 = (bf16[51,2,384]{2,1,0:T(2,128)(2,1)S(1)}, bf16[51,2,384]{2,1,0:T(2,128)(2,1)S(1)}, u32[]{:S(2)}, u32[]{:S(2)}) collective-permute-start(bf16[51,2,384]{2,1,0:T(2,128)(2,1)S(1)} %pad_maximum_fusion.packed_ref), channel_id=1, source_target_pairs={{0,2},{1,3},{2,0},{3,1},{4,6},{5,7},{6,4},{7,5},{8,10},{9,11},{10,... | collective-permute-start | bytes 235016 | tf_op jit(solution)/shard_map/ppermute | solution.py:238
  6.0 0.1 collective-permute-start.5
  6.1 1.3 %collective-permute-start.1 = (bf16[2,1024]{1,0:T(2,128)(2,1)}, bf16[2,1024]{1,0:T(2,128)(2,1)S(1)}, u32[]{:S(2)}, u32[]{:S(2)}) collective-permute-start(bf16[2,1024]{1,0:T(2,128)(2,1)} %refs_3_.1), channel_id=1, source_target_pairs={{4,0},{5,1},{6,2},{7,3},{8,4},{9,5},{10,6},{11,7},{12,8},{13,9},{1... | collective-permute-start | bytes 12296 | tf_op jit(solution)/shard_map/ppermute | solution.py:251
  7.4 0.7 %collective-permute-done.refs_0_ = bf16[2,1024]{1,0:T(2,128)(2,1)S(1)} collective-permute-done((bf16[2,1024]{1,0:T(2,128)(2,1)}, bf16[2,1024]{1,0:T(2,128)(2,1)S(1)}, u32[]{:S(2)}, u32[]{:S(2)}) %collective-permute-start) | collective-permute-done | bytes 4128 | tf_op jit(solution)/shard_map/ppermute | solution.py:251
  8.1 0.0 collective-permute-start.2
  8.1 0.3 %shift_own.1.refs_0_ = f32[8,50,128]{2,1,0:T(8,128)S(1)} custom-call(bf16[51,2,384]{2,1,0:T(2,128)(2,1)S(1)} %pad_maximum_fusion.packed_ref), custom_call_target="tpu_custom_call" | custom-call | flops 2000000000 | bytes 1048576 | tf_op jit(solution)/shard_map/shift_own/pallas_call | solution.py:84
  8.4 0.0 copy-start
  8.4 0.0 collective-permute-done.3.refs_1_
  8.4 0.6 %collective-permute-done.4.refs_2_ = bf16[51,2,384]{2,1,0:T(2,128)(2,1)S(1)} collective-permute-done((bf16[51,2,384]{2,1,0:T(2,128)(2,1)S(1)}, bf16[51,2,384]{2,1,0:T(2,128)(2,1)S(1)}, u32[]{:S(2)}, u32[]{:S(2)}) %collective-permute-start.4) | collective-permute-done | bytes 78368 | tf_op jit(solution)/shard_map/ppermute | solution.py:238
  9.0 1.4 %collective-permute-done.5.refs_3_ = bf16[51,2,384]{2,1,0:T(2,128)(2,1)S(1)} collective-permute-done((bf16[51,2,384]{2,1,0:T(2,128)(2,1)S(1)}, bf16[51,2,384]{2,1,0:T(2,128)(2,1)S(1)}, u32[]{:S(2)}, u32[]{:S(2)}) %collective-permute-start.5) | collective-permute-done | bytes 78368 | tf_op jit(solution)/shard_map/ppermute | solution.py:238
  10.4 1.0 %pick_templates.1.refs_4_ = bf16[1312,512]{1,0:T(8,128)(2,1)S(1)} custom-call(f32[8,50,128]{2,1,0:T(8,128)S(1)} %shift_own.1.refs_0_, bf16[51,2,384]{2,1,0:T(2,128)(2,1)S(1)} %collective-permute-done.3.refs_1_, bf16[51,2,384]{2,1,0:T(2,128)(2,1)S(1)} %collective-permute-done.4.refs_2_, bf16[51,2,384]{2,1,0:T(2,128)(2,1)S(1)} %collective-permute-done.5.refs_3_), custom_call_target="tpu_custom_call" | custom-call | tf_op jit(solution)/shard_map/pick_templates/pallas_call | solution.py:125
  11.4 0.4 %collective-permute-done.1.refs_1_ = bf16[2,1024]{1,0:T(2,128)(2,1)S(1)} collective-permute-done((bf16[2,1024]{1,0:T(2,128)(2,1)}, bf16[2,1024]{1,0:T(2,128)(2,1)S(1)}, u32[]{:S(2)}, u32[]{:S(2)}) %collective-permute-start.1) | collective-permute-done | bytes 4128 | tf_op jit(solution)/shard_map/ppermute | solution.py:251
  11.8 0.0 collective-permute-done.2.refs_2_
  11.8 0.0 copy-done
  11.8 2.9 %harmonic_sums.1 = f32[200,256]{1,0:T(8,128)} custom-call(bf16[2,1024]{1,0:T(2,128)(2,1)S(1)} %collective-permute-done.refs_0_, bf16[2,1024]{1,0:T(2,128)(2,1)S(1)} %collective-permute-done.1.refs_1_, bf16[2,1024]{1,0:T(2,128)(2,1)S(1)} %collective-permute-done.2.refs_2_, bf16[2,1024]{1,0:T(2,128)(2,1)S(1)} %copy-done, ...), custom_call_target="tpu_custom_call" | custom-call | tf_op jit(solution)/shard_map/harmonic_sums/pallas_call | solution.py:212
  (2 shorter events, 0.0 us)
Async XLA Ops:
  0.0 8.1 %collective-permute-start = (bf16[2,1024]{1,0:T(2,128)(2,1)}, bf16[2,1024]{1,0:T(2,128)(2,1)S(1)}, u32[]{:S(2)}, u32[]{:S(2)}) collective-permute-start(bf16[2,1024]{1,0:T(2,128)(2,1)} %refs_3_.1), channel_id=1, source_target_pairs={{12,0},{9,1},{14,2},{11,3},{13,5},{15,7},{28,16},{25,17},{30,18},{... | collective-permute-start | bytes 12296 | tf_op jit(solution)/shard_map/ppermute | solution.py:251
  3.0 5.4 %collective-permute-start.3 = (bf16[51,2,384]{2,1,0:T(2,128)(2,1)S(1)}, bf16[51,2,384]{2,1,0:T(2,128)(2,1)S(1)}, u32[]{:S(2)}, u32[]{:S(2)}) collective-permute-start(bf16[51,2,384]{2,1,0:T(2,128)(2,1)S(1)} %pad_maximum_fusion.packed_ref), channel_id=1, source_target_pairs={{0,1},{1,0},{2,3},{3,2},{4,5},{5,4},{6,7},{7,6},{8,9},{9,8},{10,11... | collective-permute-start | bytes 235016 | tf_op jit(solution)/shard_map/ppermute | solution.py:238
  3.5 5.5 %collective-permute-start.4 = (bf16[51,2,384]{2,1,0:T(2,128)(2,1)S(1)}, bf16[51,2,384]{2,1,0:T(2,128)(2,1)S(1)}, u32[]{:S(2)}, u32[]{:S(2)}) collective-permute-start(bf16[51,2,384]{2,1,0:T(2,128)(2,1)S(1)} %pad_maximum_fusion.packed_ref), channel_id=1, source_target_pairs={{0,2},{1,3},{2,0},{3,1},{4,6},{5,7},{6,4},{7,5},{8,10},{9,11},{10,... | collective-permute-start | bytes 235016 | tf_op jit(solution)/shard_map/ppermute | solution.py:238
  6.0 4.3 %collective-permute-start.5 = (bf16[51,2,384]{2,1,0:T(2,128)(2,1)S(1)}, bf16[51,2,384]{2,1,0:T(2,128)(2,1)S(1)}, u32[]{:S(2)}, u32[]{:S(2)}) collective-permute-start(bf16[51,2,384]{2,1,0:T(2,128)(2,1)S(1)} %pad_maximum_fusion.packed_ref), channel_id=1, source_target_pairs={{0,3},{1,2},{2,1},{3,0},{4,7},{5,6},{6,5},{7,4},{8,11},{9,10},{10,... | collective-permute-start | bytes 235016 | tf_op jit(solution)/shard_map/ppermute | solution.py:238
  6.1 5.7 %collective-permute-start.1 = (bf16[2,1024]{1,0:T(2,128)(2,1)}, bf16[2,1024]{1,0:T(2,128)(2,1)S(1)}, u32[]{:S(2)}, u32[]{:S(2)}) collective-permute-start(bf16[2,1024]{1,0:T(2,128)(2,1)} %refs_3_.1), channel_id=1, source_target_pairs={{4,0},{5,1},{6,2},{7,3},{8,4},{9,5},{10,6},{11,7},{12,8},{13,9},{1... | collective-permute-start | bytes 12296 | tf_op jit(solution)/shard_map/ppermute | solution.py:251
  8.1 3.7 %collective-permute-start.2 = (bf16[2,1024]{1,0:T(2,128)(2,1)S(1)}, bf16[2,1024]{1,0:T(2,128)(2,1)S(1)}, u32[]{:S(2)}, u32[]{:S(2)}) collective-permute-start(bf16[2,1024]{1,0:T(2,128)(2,1)S(1)} %collective-permute-done.refs_0_), channel_id=1, source_target_pairs={{0,1},{1,0},{2,3},{3,2},{4,5},{5,4},{6,7},{7,6},{8,9},{9,8},{10,11... | collective-permute-start | bytes 12296 | tf_op jit(solution)/shard_map/ppermute | solution.py:238
  8.4 3.5 %copy-start = (bf16[2,1024]{1,0:T(2,128)(2,1)S(1)}, bf16[2,1024]{1,0:T(2,128)(2,1)}, u32[]{:S(2)}) copy-start(bf16[2,1024]{1,0:T(2,128)(2,1)} %refs_3_.1) | copy-start | bytes 12292

commit v7 on v6

--- a/solution.py
+++ b/solution.py
@@ -253,7 +253,7 @@
 
 
 def gathered_templates(packed):
-    return [shift_own(packed)] + [swapped(packed, mask) for mask in range(1, lax.axis_size("acc"))]
+    return [shift_own(packed)] + [swapped(packed, mask) for mask in range(lax.axis_size("acc") - 1, 0, -1)]
 
 
 def shards(spectrum, templates, offsets):
@@ -261,7 +261,7 @@
     rows = acc_count * templates.shape[1]
     slabs = gathered_slabs(spectrum)
     held = gathered_templates(pack_templates(jnp.transpose(templates, (1, 0, 2)), offsets))
-    picked = pick_templates(held, range(acc_count), rows)
+    picked = pick_templates(held, [0, *range(acc_count - 1, 0, -1)], rows)
     return harmonic_sums(slabs, picked, rows, spectrum.shape[1] // acc_count)
 
 

time: 15 us -> 14.9 us (level)
  transfers between devices with their start and end apart: 6 -> 6, of which waited for: 4 -> 3; matrix products, arithmetic and copies ran while one was open for 11% -> 11% of each run, Pallas kernels for 9% -> 9%
where the time goes in v7:
time: 14.9 us; the launch traced here: 14.7 us
  starting transfers between devices  5.68 us (38%)
  Pallas kernels  4.21 us (28%)
  waiting for transfers between devices  3.11 us (21%)
  other arithmetic  1.66 us (11%)
    ppermute x4, starting transfers between devices, swapped(): lax.ppermute(value, 'acc', [(i, i ^ mask) for i in range(lax.axis_size('a...  3.12 us
    pallas_call x1, Pallas kernels, harmonic_sums(): pl.pallas_call(functools.partial(harmonic_kernel, n_slabs=len(slabs), row...  2.93 us
    ppermute x2, starting transfers between devices, gathered_slabs(): fetched.append(lax.ppermute(spectrum, ('freq', 'acc'), pairs))  2.56 us
    ppermute x4, waiting for transfers between devices, swapped(): lax.ppermute(value, 'acc', [(i, i ^ mask) for i in range(lax.axis_size('a...  1.97 us
    ppermute x2, waiting for transfers between devices, gathered_slabs(): fetched.append(lax.ppermute(spectrum, ('freq', 'acc'), pairs))  1.14 us
    pallas_call x1, Pallas kernels, pick_templates(): pl.pallas_call(functools.partial(pick_kernel, masks=masks, shard_rows=sha...  1.02 us
    concatenate x1, other arithmetic, pack_templates(): return jnp.concatenate([templates, wide.astype(templates.dtype)], axis=0)  1 us
    another operation x1, other arithmetic  0.66 us
  transfers between devices with their start and end apart: 6, of which 3 were waited for; matrix products, arithmetic and copies ran while one was open for 11% of the time, Pallas kernels for 9%

profile of v7, /device:TPU:0, one launch (start us, length us, event | category | flops | bytes accessed | tf_op | source)
XLA Modules:
  0.0 14.7 jit_solution(360640392499771108)
XLA Ops:
  0.0 1.3 %collective-permute-start = (bf16[2,1024]{1,0:T(2,128)(2,1)}, bf16[2,1024]{1,0:T(2,128)(2,1)S(1)}, u32[]{:S(2)}, u32[]{:S(2)}) collective-permute-start(bf16[2,1024]{1,0:T(2,128)(2,1)} %refs_3_.1), channel_id=1, source_target_pairs={{12,0},{9,1},{14,2},{11,3},{13,5},{15,7},{28,16},{25,17},{30,18},{... | collective-permute-start | bytes 12296 | tf_op jit(solution)/shard_map/ppermute | solution.py:251
  1.3 0.7 %convert.4 = bf16[50]{0:T(256)(128)(2,1)S(1)} convert(s32[50]{0:T(128)} %param.5) | non-fusion elementwise | flops 50 | bytes 300 | tf_op jit(solution)/shard_map/convert
  2.0 1.0 %pad_maximum_fusion.packed_ref = bf16[51,2,384]{2,1,0:T(2,128)(2,1)S(1)} fusion(bf16[1,2,384]{2,1,0:T(2,128)(2,1)S(1)} %broadcast_in_dim.3, bf16[50,2,384]{2,1,0:T(2,128)(2,1)} %bitcast.1), kind=kLoop, calls=%fused_computation | loop fusion | flops 39168 | bytes 156672 | tf_op jit(solution)/shard_map/concatenate | solution.py:41
  3.0 2.4 %collective-permute-start.3 = (bf16[51,2,384]{2,1,0:T(2,128)(2,1)S(1)}, bf16[51,2,384]{2,1,0:T(2,128)(2,1)S(1)}, u32[]{:S(2)}, u32[]{:S(2)}) collective-permute-start(bf16[51,2,384]{2,1,0:T(2,128)(2,1)S(1)} %pad_maximum_fusion.packed_ref), channel_id=1, source_target_pairs={{0,3},{1,2},{2,1},{3,0},{4,7},{5,6},{6,5},{7,4},{8,11},{9,10},{10,... | collective-permute-start | bytes 235016 | tf_op jit(solution)/shard_map/ppermute | solution.py:238
  5.4 0.6 %collective-permute-start.4 = (bf16[51,2,384]{2,1,0:T(2,128)(2,1)S(1)}, bf16[51,2,384]{2,1,0:T(2,128)(2,1)S(1)}, u32[]{:S(2)}, u32[]{:S(2)}) collective-permute-start(bf16[51,2,384]{2,1,0:T(2,128)(2,1)S(1)} %pad_maximum_fusion.packed_ref), channel_id=1, source_target_pairs={{0,2},{1,3},{2,0},{3,1},{4,6},{5,7},{6,4},{7,5},{8,10},{9,11},{10,... | collective-permute-start | bytes 235016 | tf_op jit(solution)/shard_map/ppermute | solution.py:238
  6.0 0.0 collective-permute-start.5
  6.1 1.3 %collective-permute-start.1 = (bf16[2,1024]{1,0:T(2,128)(2,1)}, bf16[2,1024]{1,0:T(2,128)(2,1)S(1)}, u32[]{:S(2)}, u32[]{:S(2)}) collective-permute-start(bf16[2,1024]{1,0:T(2,128)(2,1)} %refs_3_.1), channel_id=1, source_target_pairs={{4,0},{5,1},{6,2},{7,3},{8,4},{9,5},{10,6},{11,7},{12,8},{13,9},{1... | collective-permute-start | bytes 12296 | tf_op jit(solution)/shard_map/ppermute | solution.py:251
  7.4 0.7 %collective-permute-done.refs_0_ = bf16[2,1024]{1,0:T(2,128)(2,1)S(1)} collective-permute-done((bf16[2,1024]{1,0:T(2,128)(2,1)}, bf16[2,1024]{1,0:T(2,128)(2,1)S(1)}, u32[]{:S(2)}, u32[]{:S(2)}) %collective-permute-start) | collective-permute-done | bytes 4128 | tf_op jit(solution)/shard_map/ppermute | solution.py:251
  8.1 0.0 collective-permute-start.2
  8.1 0.3 %shift_own.1.refs_0_ = f32[8,50,128]{2,1,0:T(8,128)S(1)} custom-call(bf16[51,2,384]{2,1,0:T(2,128)(2,1)S(1)} %pad_maximum_fusion.packed_ref), custom_call_target="tpu_custom_call" | custom-call | flops 2000000000 | bytes 1048576 | tf_op jit(solution)/shard_map/shift_own/pallas_call | solution.py:84
  8.4 0.0 copy-start
  8.4 0.0 collective-permute-done.3.refs_1_
  8.4 2.0 %collective-permute-done.4.refs_2_ = bf16[51,2,384]{2,1,0:T(2,128)(2,1)S(1)} collective-permute-done((bf16[51,2,384]{2,1,0:T(2,128)(2,1)S(1)}, bf16[51,2,384]{2,1,0:T(2,128)(2,1)S(1)}, u32[]{:S(2)}, u32[]{:S(2)}) %collective-permute-start.4) | collective-permute-done | bytes 78368 | tf_op jit(solution)/shard_map/ppermute | solution.py:238
  10.4 0.0 collective-permute-done.5.refs_3_
  10.4 1.0 %pick_templates.1.refs_4_ = bf16[1312,512]{1,0:T(8,128)(2,1)S(1)} custom-call(f32[8,50,128]{2,1,0:T(8,128)S(1)} %shift_own.1.refs_0_, bf16[51,2,384]{2,1,0:T(2,128)(2,1)S(1)} %collective-permute-done.3.refs_1_, bf16[51,2,384]{2,1,0:T(2,128)(2,1)S(1)} %collective-permute-done.4.refs_2_, bf16[51,2,384]{2,1,0:T(2,128)(2,1)S(1)} %collective-permute-done.5.refs_3_), custom_call_target="tpu_custom_call" | custom-call | tf_op jit(solution)/shard_map/pick_templates/pallas_call | solution.py:125
  11.4 0.4 %collective-permute-done.1.refs_1_ = bf16[2,1024]{1,0:T(2,128)(2,1)S(1)} collective-permute-done((bf16[2,1024]{1,0:T(2,128)(2,1)}, bf16[2,1024]{1,0:T(2,128)(2,1)S(1)}, u32[]{:S(2)}, u32[]{:S(2)}) %collective-permute-start.1) | collective-permute-done | bytes 4128 | tf_op jit(solution)/shard_map/ppermute | solution.py:251
  11.8 0.0 collective-permute-done.2.refs_2_
  11.8 0.0 copy-done
  11.8 2.9 %harmonic_sums.1 = f32[200,256]{1,0:T(8,128)} custom-call(bf16[2,1024]{1,0:T(2,128)(2,1)S(1)} %collective-permute-done.refs_0_, bf16[2,1024]{1,0:T(2,128)(2,1)S(1)} %collective-permute-done.1.refs_1_, bf16[2,1024]{1,0:T(2,128)(2,1)S(1)} %collective-permute-done.2.refs_2_, bf16[2,1024]{1,0:T(2,128)(2,1)S(1)} %copy-done, ...), custom_call_target="tpu_custom_call" | custom-call | tf_op jit(solution)/shard_map/harmonic_sums/pallas_call | solution.py:212
  (2 shorter events, 0.0 us)
Async XLA Ops:
  0.0 8.1 %collective-permute-start = (bf16[2,1024]{1,0:T(2,128)(2,1)}, bf16[2,1024]{1,0:T(2,128)(2,1)S(1)}, u32[]{:S(2)}, u32[]{:S(2)}) collective-permute-start(bf16[2,1024]{1,0:T(2,128)(2,1)} %refs_3_.1), channel_id=1, source_target_pairs={{12,0},{9,1},{14,2},{11,3},{13,5},{15,7},{28,16},{25,17},{30,18},{... | collective-permute-start | bytes 12296 | tf_op jit(solution)/shard_map/ppermute | solution.py:251
  3.0 5.4 %collective-permute-start.3 = (bf16[51,2,384]{2,1,0:T(2,128)(2,1)S(1)}, bf16[51,2,384]{2,1,0:T(2,128)(2,1)S(1)}, u32[]{:S(2)}, u32[]{:S(2)}) collective-permute-start(bf16[51,2,384]{2,1,0:T(2,128)(2,1)S(1)} %pad_maximum_fusion.packed_ref), channel_id=1, source_target_pairs={{0,3},{1,2},{2,1},{3,0},{4,7},{5,6},{6,5},{7,4},{8,11},{9,10},{10,... | collective-permute-start | bytes 235016 | tf_op jit(solution)/shard_map/ppermute | solution.py:238
  5.4 4.9 %collective-permute-start.4 = (bf16[51,2,384]{2,1,0:T(2,128)(2,1)S(1)}, bf16[51,2,384]{2,1,0:T(2,128)(2,1)S(1)}, u32[]{:S(2)}, u32[]{:S(2)}) collective-permute-start(bf16[51,2,384]{2,1,0:T(2,128)(2,1)S(1)} %pad_maximum_fusion.packed_ref), channel_id=1, source_target_pairs={{0,2},{1,3},{2,0},{3,1},{4,6},{5,7},{6,4},{7,5},{8,10},{9,11},{10,... | collective-permute-start | bytes 235016 | tf_op jit(solution)/shard_map/ppermute | solution.py:238
  6.0 4.3 %collective-permute-start.5 = (bf16[51,2,384]{2,1,0:T(2,128)(2,1)S(1)}, bf16[51,2,384]{2,1,0:T(2,128)(2,1)S(1)}, u32[]{:S(2)}, u32[]{:S(2)}) collective-permute-start(bf16[51,2,384]{2,1,0:T(2,128)(2,1)S(1)} %pad_maximum_fusion.packed_ref), channel_id=1, source_target_pairs={{0,1},{1,0},{2,3},{3,2},{4,5},{5,4},{6,7},{7,6},{8,9},{9,8},{10,11... | collective-permute-start | bytes 235016 | tf_op jit(solution)/shard_map/ppermute | solution.py:238
  6.1 5.7 %collective-permute-start.1 = (bf16[2,1024]{1,0:T(2,128)(2,1)}, bf16[2,1024]{1,0:T(2,128)(2,1)S(1)}, u32[]{:S(2)}, u32[]{:S(2)}) collective-permute-start(bf16[2,1024]{1,0:T(2,128)(2,1)} %refs_3_.1), channel_id=1, source_target_pairs={{4,0},{5,1},{6,2},{7,3},{8,4},{9,5},{10,6},{11,7},{12,8},{13,9},{1... | collective-permute-start | bytes 12296 | tf_op jit(solution)/shard_map/ppermute | solution.py:251
  8.1 3.7 %collective-permute-start.2 = (bf16[2,1024]{1,0:T(2,128)(2,1)S(1)}, bf16[2,1024]{1,0:T(2,128)(2,1)S(1)}, u32[]{:S(2)}, u32[]{:S(2)}) collective-permute-start(bf16[2,1024]{1,0:T(2,128)(2,1)S(1)} %collective-permute-done.refs_0_), channel_id=1, source_target_pairs={{0,1},{1,0},{2,3},{3,2},{4,5},{5,4},{6,7},{7,6},{8,9},{9,8},{10,11... | collective-permute-start | bytes 12296 | tf_op jit(solution)/shard_map/ppermute | solution.py:238
  8.4 3.4 %copy-start = (bf16[2,1024]{1,0:T(2,128)(2,1)S(1)}, bf16[2,1024]{1,0:T(2,128)(2,1)}, u32[]{:S(2)}) copy-start(bf16[2,1024]{1,0:T(2,128)(2,1)} %refs_3_.1) | copy-start | bytes 12292

commit v8 on v7

--- a/solution.py
+++ b/solution.py
@@ -156,7 +156,6 @@
 
     lane = lax.broadcasted_iota(jnp.int32, (16, LANES), 1)
     sublane = lax.broadcasted_iota(jnp.int32, (16, LANES), 0)
-    total[...] = jnp.zeros_like(total)
     at = [0]
     for _, count in blocks:
         at.append(at[-1] + 2 * count)
@@ -198,7 +197,10 @@
         real = with_real[:count] - with_imag[count:]
         imag = with_imag[:count] + with_real[count:]
         power = (real * real + imag * imag).astype(jnp.bfloat16)
-        total[start : start + count, :] += power.astype(jnp.float32)
+        if harmonic == 1:
+            total[...] = power.astype(jnp.float32)
+        else:
+            total[start : start + count, :] += power.astype(jnp.float32)
 
     for harmonic in range(1, H + 1):
         build(harmonic)

time: 14.9 us -> 14.9 us (level)
  no operation moved by 1% of the time
where the time goes in v8:
time: 14.9 us; the launch traced here: 14.7 us
  starting transfers between devices  5.68 us (38%)
  Pallas kernels  4.21 us (28%)
  waiting for transfers between devices  3.11 us (21%)
  other arithmetic  1.66 us (11%)
    ppermute x4, starting transfers between devices, swapped(): lax.ppermute(value, 'acc', [(i, i ^ mask) for i in range(lax.axis_size('a...  3.12 us
    pallas_call x1, Pallas kernels, harmonic_sums(): pl.pallas_call(functools.partial(harmonic_kernel, n_slabs=len(slabs), row...  2.93 us
    ppermute x2, starting transfers between devices, gathered_slabs(): fetched.append(lax.ppermute(spectrum, ('freq', 'acc'), pairs))  2.56 us
    ppermute x4, waiting for transfers between devices, swapped(): lax.ppermute(value, 'acc', [(i, i ^ mask) for i in range(lax.axis_size('a...  1.97 us
    ppermute x2, waiting for transfers between devices, gathered_slabs(): fetched.append(lax.ppermute(spectrum, ('freq', 'acc'), pairs))  1.14 us
    pallas_call x1, Pallas kernels, pick_templates(): pl.pallas_call(functools.partial(pick_kernel, masks=masks, shard_rows=sha...  1.02 us
    concatenate x1, other arithmetic, pack_templates(): return jnp.concatenate([templates, wide.astype(templates.dtype)], axis=0)  1 us
    another operation x1, other arithmetic  0.66 us
  transfers between devices with their start and end apart: 6, of which 3 were waited for; matrix products, arithmetic and copies ran while one was open for 11% of the time, Pallas kernels for 9%

profile of v8, /device:TPU:0, one launch (start us, length us, event | category | flops | bytes accessed | tf_op | source)
XLA Modules:
  0.0 14.7 jit_solution(360640392499771108)
XLA Ops:
  0.0 1.3 %collective-permute-start = (bf16[2,1024]{1,0:T(2,128)(2,1)}, bf16[2,1024]{1,0:T(2,128)(2,1)S(1)}, u32[]{:S(2)}, u32[]{:S(2)}) collective-permute-start(bf16[2,1024]{1,0:T(2,128)(2,1)} %refs_3_.1), channel_id=1, source_target_pairs={{12,0},{9,1},{14,2},{11,3},{13,5},{15,7},{28,16},{25,17},{30,18},{... | collective-permute-start | bytes 12296 | tf_op jit(solution)/shard_map/ppermute | solution.py:253
  1.3 0.7 %convert.4 = bf16[50]{0:T(256)(128)(2,1)S(1)} convert(s32[50]{0:T(128)} %param.5) | non-fusion elementwise | flops 50 | bytes 300 | tf_op jit(solution)/shard_map/convert
  2.0 1.0 %pad_maximum_fusion.packed_ref = bf16[51,2,384]{2,1,0:T(2,128)(2,1)S(1)} fusion(bf16[1,2,384]{2,1,0:T(2,128)(2,1)S(1)} %broadcast_in_dim.3, bf16[50,2,384]{2,1,0:T(2,128)(2,1)} %bitcast.1), kind=kLoop, calls=%fused_computation | loop fusion | flops 39168 | bytes 156672 | tf_op jit(solution)/shard_map/concatenate | solution.py:41
  3.0 2.4 %collective-permute-start.3 = (bf16[51,2,384]{2,1,0:T(2,128)(2,1)S(1)}, bf16[51,2,384]{2,1,0:T(2,128)(2,1)S(1)}, u32[]{:S(2)}, u32[]{:S(2)}) collective-permute-start(bf16[51,2,384]{2,1,0:T(2,128)(2,1)S(1)} %pad_maximum_fusion.packed_ref), channel_id=1, source_target_pairs={{0,3},{1,2},{2,1},{3,0},{4,7},{5,6},{6,5},{7,4},{8,11},{9,10},{10,... | collective-permute-start | bytes 235016 | tf_op jit(solution)/shard_map/ppermute | solution.py:240
  5.4 0.6 %collective-permute-start.4 = (bf16[51,2,384]{2,1,0:T(2,128)(2,1)S(1)}, bf16[51,2,384]{2,1,0:T(2,128)(2,1)S(1)}, u32[]{:S(2)}, u32[]{:S(2)}) collective-permute-start(bf16[51,2,384]{2,1,0:T(2,128)(2,1)S(1)} %pad_maximum_fusion.packed_ref), channel_id=1, source_target_pairs={{0,2},{1,3},{2,0},{3,1},{4,6},{5,7},{6,4},{7,5},{8,10},{9,11},{10,... | collective-permute-start | bytes 235016 | tf_op jit(solution)/shard_map/ppermute | solution.py:240
  6.0 0.0 collective-permute-start.5
  6.1 1.3 %collective-permute-start.1 = (bf16[2,1024]{1,0:T(2,128)(2,1)}, bf16[2,1024]{1,0:T(2,128)(2,1)S(1)}, u32[]{:S(2)}, u32[]{:S(2)}) collective-permute-start(bf16[2,1024]{1,0:T(2,128)(2,1)} %refs_3_.1), channel_id=1, source_target_pairs={{4,0},{5,1},{6,2},{7,3},{8,4},{9,5},{10,6},{11,7},{12,8},{13,9},{1... | collective-permute-start | bytes 12296 | tf_op jit(solution)/shard_map/ppermute | solution.py:253
  7.4 0.7 %collective-permute-done.refs_0_ = bf16[2,1024]{1,0:T(2,128)(2,1)S(1)} collective-permute-done((bf16[2,1024]{1,0:T(2,128)(2,1)}, bf16[2,1024]{1,0:T(2,128)(2,1)S(1)}, u32[]{:S(2)}, u32[]{:S(2)}) %collective-permute-start) | collective-permute-done | bytes 4128 | tf_op jit(solution)/shard_map/ppermute | solution.py:253
  8.1 0.0 collective-permute-start.2
  8.1 0.3 %shift_own.1.refs_0_ = f32[8,50,128]{2,1,0:T(8,128)S(1)} custom-call(bf16[51,2,384]{2,1,0:T(2,128)(2,1)S(1)} %pad_maximum_fusion.packed_ref), custom_call_target="tpu_custom_call" | custom-call | flops 2000000000 | bytes 1048576 | tf_op jit(solution)/shard_map/shift_own/pallas_call | solution.py:84
  8.4 0.0 copy-start
  8.4 0.0 collective-permute-done.3.refs_1_
  8.4 2.0 %collective-permute-done.4.refs_2_ = bf16[51,2,384]{2,1,0:T(2,128)(2,1)S(1)} collective-permute-done((bf16[51,2,384]{2,1,0:T(2,128)(2,1)S(1)}, bf16[51,2,384]{2,1,0:T(2,128)(2,1)S(1)}, u32[]{:S(2)}, u32[]{:S(2)}) %collective-permute-start.4) | collective-permute-done | bytes 78368 | tf_op jit(solution)/shard_map/ppermute | solution.py:240
  10.4 0.0 collective-permute-done.5.refs_3_
  10.4 1.0 %pick_templates.1.refs_4_ = bf16[1312,512]{1,0:T(8,128)(2,1)S(1)} custom-call(f32[8,50,128]{2,1,0:T(8,128)S(1)} %shift_own.1.refs_0_, bf16[51,2,384]{2,1,0:T(2,128)(2,1)S(1)} %collective-permute-done.3.refs_1_, bf16[51,2,384]{2,1,0:T(2,128)(2,1)S(1)} %collective-permute-done.4.refs_2_, bf16[51,2,384]{2,1,0:T(2,128)(2,1)S(1)} %collective-permute-done.5.refs_3_), custom_call_target="tpu_custom_call" | custom-call | tf_op jit(solution)/shard_map/pick_templates/pallas_call | solution.py:125
  11.4 0.4 %collective-permute-done.1.refs_1_ = bf16[2,1024]{1,0:T(2,128)(2,1)S(1)} collective-permute-done((bf16[2,1024]{1,0:T(2,128)(2,1)}, bf16[2,1024]{1,0:T(2,128)(2,1)S(1)}, u32[]{:S(2)}, u32[]{:S(2)}) %collective-permute-start.1) | collective-permute-done | bytes 4128 | tf_op jit(solution)/shard_map/ppermute | solution.py:253
  11.8 0.0 collective-permute-done.2.refs_2_
  11.8 0.0 copy-done
  11.8 2.9 %harmonic_sums.1 = f32[200,256]{1,0:T(8,128)} custom-call(bf16[2,1024]{1,0:T(2,128)(2,1)S(1)} %collective-permute-done.refs_0_, bf16[2,1024]{1,0:T(2,128)(2,1)S(1)} %collective-permute-done.1.refs_1_, bf16[2,1024]{1,0:T(2,128)(2,1)S(1)} %collective-permute-done.2.refs_2_, bf16[2,1024]{1,0:T(2,128)(2,1)S(1)} %copy-done, ...), custom_call_target="tpu_custom_call" | custom-call | tf_op jit(solution)/shard_map/harmonic_sums/pallas_call | solution.py:214
  (2 shorter events, 0.0 us)
Async XLA Ops:
  0.0 8.1 %collective-permute-start = (bf16[2,1024]{1,0:T(2,128)(2,1)}, bf16[2,1024]{1,0:T(2,128)(2,1)S(1)}, u32[]{:S(2)}, u32[]{:S(2)}) collective-permute-start(bf16[2,1024]{1,0:T(2,128)(2,1)} %refs_3_.1), channel_id=1, source_target_pairs={{12,0},{9,1},{14,2},{11,3},{13,5},{15,7},{28,16},{25,17},{30,18},{... | collective-permute-start | bytes 12296 | tf_op jit(solution)/shard_map/ppermute | solution.py:253
  3.0 5.4 %collective-permute-start.3 = (bf16[51,2,384]{2,1,0:T(2,128)(2,1)S(1)}, bf16[51,2,384]{2,1,0:T(2,128)(2,1)S(1)}, u32[]{:S(2)}, u32[]{:S(2)}) collective-permute-start(bf16[51,2,384]{2,1,0:T(2,128)(2,1)S(1)} %pad_maximum_fusion.packed_ref), channel_id=1, source_target_pairs={{0,3},{1,2},{2,1},{3,0},{4,7},{5,6},{6,5},{7,4},{8,11},{9,10},{10,... | collective-permute-start | bytes 235016 | tf_op jit(solution)/shard_map/ppermute | solution.py:240
  5.4 4.9 %collective-permute-start.4 = (bf16[51,2,384]{2,1,0:T(2,128)(2,1)S(1)}, bf16[51,2,384]{2,1,0:T(2,128)(2,1)S(1)}, u32[]{:S(2)}, u32[]{:S(2)}) collective-permute-start(bf16[51,2,384]{2,1,0:T(2,128)(2,1)S(1)} %pad_maximum_fusion.packed_ref), channel_id=1, source_target_pairs={{0,2},{1,3},{2,0},{3,1},{4,6},{5,7},{6,4},{7,5},{8,10},{9,11},{10,... | collective-permute-start | bytes 235016 | tf_op jit(solution)/shard_map/ppermute | solution.py:240
  6.0 4.3 %collective-permute-start.5 = (bf16[51,2,384]{2,1,0:T(2,128)(2,1)S(1)}, bf16[51,2,384]{2,1,0:T(2,128)(2,1)S(1)}, u32[]{:S(2)}, u32[]{:S(2)}) collective-permute-start(bf16[51,2,384]{2,1,0:T(2,128)(2,1)S(1)} %pad_maximum_fusion.packed_ref), channel_id=1, source_target_pairs={{0,1},{1,0},{2,3},{3,2},{4,5},{5,4},{6,7},{7,6},{8,9},{9,8},{10,11... | collective-permute-start | bytes 235016 | tf_op jit(solution)/shard_map/ppermute | solution.py:240
  6.1 5.7 %collective-permute-start.1 = (bf16[2,1024]{1,0:T(2,128)(2,1)}, bf16[2,1024]{1,0:T(2,128)(2,1)S(1)}, u32[]{:S(2)}, u32[]{:S(2)}) collective-permute-start(bf16[2,1024]{1,0:T(2,128)(2,1)} %refs_3_.1), channel_id=1, source_target_pairs={{4,0},{5,1},{6,2},{7,3},{8,4},{9,5},{10,6},{11,7},{12,8},{13,9},{1... | collective-permute-start | bytes 12296 | tf_op jit(solution)/shard_map/ppermute | solution.py:253
  8.1 3.7 %collective-permute-start.2 = (bf16[2,1024]{1,0:T(2,128)(2,1)S(1)}, bf16[2,1024]{1,0:T(2,128)(2,1)S(1)}, u32[]{:S(2)}, u32[]{:S(2)}) collective-permute-start(bf16[2,1024]{1,0:T(2,128)(2,1)S(1)} %collective-permute-done.refs_0_), channel_id=1, source_target_pairs={{0,1},{1,0},{2,3},{3,2},{4,5},{5,4},{6,7},{7,6},{8,9},{9,8},{10,11... | collective-permute-start | bytes 12296 | tf_op jit(solution)/shard_map/ppermute | solution.py:240
  8.4 3.4 %copy-start = (bf16[2,1024]{1,0:T(2,128)(2,1)S(1)}, bf16[2,1024]{1,0:T(2,128)(2,1)}, u32[]{:S(2)}) copy-start(bf16[2,1024]{1,0:T(2,128)(2,1)} %refs_3_.1) | copy-start | bytes 12292
